TPU v7x, 256 devices: a whole 4x4x8 slice. The times are simulated.
256 devices in a mesh: dp: 16 (over z_hi, y), tensor: 8 (over z_lo, x), probe: 2 (over core).
Axes of the slice: x: 4, y: 4, z: 8 (z_hi: 4, z_lo: 2; z = z_hi * 2 + z_lo), core: 2. Of those that a mesh axis runs over, the one named last changes fastest.
Arguments:
- tokens: bfloat16 [2048, 4096], P('dp'), may hold values from -6 to 6
- cotangent: bfloat16 [2048, 4096], P('dp'), may hold values from -6 to 6
- gate_weight: bfloat16 [4096, 14336], P('dp', ('tensor', 'probe')), may hold values from -0.09375 to 0.09375
- up_weight: bfloat16 [4096, 14336], P('dp', ('tensor', 'probe')), may hold values from -0.09375 to 0.09375
- down_weight: bfloat16 [14336, 4096], P(('tensor', 'probe'), 'dp'), may hold values from -0.046875 to 0.046875
- probe_seeds: int32 [2], replicated, may hold values from 0 to 1073741823
Outputs:
- tangent: bfloat16 [2, 2048, 4096], P(None, 'dp', ('tensor', 'probe'))
- curvature: float32 [2, 2048], P(None, 'dp')
All inputs are finite; a program needn't handle non-finite values.
Results may differ from a plain program's by a relative error of at most 0.023.
Values may be sent and summed in bfloat16 or wider, within the bound.
A program may use at most 128 MiB of HBM per device.

v0:
```python
import jax
import jax.numpy as jnp
from jax import lax
from jax.sharding import PartitionSpec as P

D = 4096
FF = 14336


def upper_bits(number, shift_by):
    return jnp.right_shift(number, shift_by) & (1 << 32 - shift_by) - 1


def rademacher(seed_value, salt, row_ids, col_ids, col_total, factor):
    flat_index = row_ids[:, None] * col_total + col_ids[None, :]
    hashed = flat_index * jnp.int32(-1640531535) + (seed_value + salt * 40503)
    hashed = hashed ^ upper_bits(hashed, 16)
    hashed = hashed * jnp.int32(739982445)
    hashed = hashed ^ upper_bits(hashed, 13)
    hashed = hashed * jnp.int32(695872825)
    hashed = hashed ^ upper_bits(hashed, 16)
    signs = 1 - 2 * upper_bits(hashed, 31)
    return (signs.astype(jnp.float32) * factor).astype(jnp.bfloat16)


def probe_stack(probe_seeds, salt, row_ids, col_ids, col_total, factor):
    return jnp.stack(
        [
            rademacher(probe_seeds[probe_index], salt, row_ids, col_ids, col_total, factor)
            for probe_index in range(probe_seeds.shape[0])
        ]
    )


def silu_terms(gate_pre):
    sigmoid_val = jax.nn.sigmoid(gate_pre)
    silu_val = gate_pre * sigmoid_val
    silu_slope = sigmoid_val * (1.0 + gate_pre * (1.0 - sigmoid_val))
    silu_bend = sigmoid_val * (1.0 - sigmoid_val) * (2.0 + gate_pre * (1.0 - 2.0 * sigmoid_val))
    return (silu_val, silu_slope, silu_bend)


def on_device(tokens, cotangent, gate_weight, up_weight, down_weight, probe_seeds):
    in_factor = D ** (-0.5)
    out_factor = FF ** (-0.5)
    unit_count = gate_weight.shape[1]
    unit_ids = lax.axis_index(("tensor", "probe")) * unit_count + jnp.arange(
        unit_count, dtype=jnp.int32
    )

    def project_rows(weight_piece, salt):
        row_count = weight_piece.shape[0]
        row_ids = jnp.arange(row_count, dtype=jnp.int32)
        directions = probe_stack(probe_seeds, salt, row_ids, unit_ids, FF, in_factor)
        plain = jnp.dot(tokens, weight_piece, preferred_element_type=jnp.float32)
        along = jnp.einsum("tn,pnf->ptf", tokens, directions, preferred_element_type=jnp.float32)
        return (plain, along)

    plain, along = project_rows(lax.all_gather(gate_weight, "dp", axis=0, tiled=True), 1)
    gate_pre = plain
    gate_dir = along
    plain, along = project_rows(lax.all_gather(up_weight, "dp", axis=0, tiled=True), 2)
    up_pre = plain
    up_dir = along
    silu_val, silu_slope, silu_bend = silu_terms(gate_pre)
    hidden = (silu_val * up_pre).astype(jnp.bfloat16)
    hidden_dir = silu_slope * gate_dir * up_pre + silu_val * up_dir
    hidden_dir_low = hidden_dir.astype(jnp.bfloat16)
    hidden_curv = silu_bend * gate_dir * gate_dir * up_pre + 2.0 * silu_slope * gate_dir * up_dir
    piece = lax.all_gather(down_weight, "dp", axis=1, tiled=True)
    col_count = piece.shape[1]
    col_ids = jnp.arange(col_count, dtype=jnp.int32)
    directions = probe_stack(probe_seeds, 3, unit_ids, col_ids, D, out_factor)
    plain = jnp.einsum("tn,fn->tf", cotangent, piece, preferred_element_type=jnp.float32)
    along = jnp.einsum("tn,pfn->ptf", cotangent, directions, preferred_element_type=jnp.float32)
    plain, along = (plain, along)
    piece = lax.all_gather(down_weight, "dp", axis=1, tiled=True)
    col_count = piece.shape[1]
    col_ids = jnp.arange(col_count, dtype=jnp.int32)
    directions = probe_stack(probe_seeds, 3, unit_ids, col_ids, D, out_factor)
    first_term = jnp.einsum(
        "ptf,fn->ptn", hidden_dir_low, piece, preferred_element_type=jnp.float32
    )
    tangent_terms = first_term + jnp.einsum(
        "tf,pfn->ptn", hidden, directions, preferred_element_type=jnp.float32
    )
    local_curv = jnp.sum(plain[None] * hidden_curv + 2.0 * along * hidden_dir, axis=2)
    curvature = lax.psum(local_curv, ("tensor", "probe")) * out_factor
    tangent = lax.psum_scatter(
        tangent_terms.astype(jnp.bfloat16), ("tensor", "probe"), scatter_dimension=2, tiled=True
    )
    return (tangent, curvature)


def solution(mesh):
    return jax.shard_map(
        on_device,
        mesh=mesh,
        in_specs=(
            P("dp", None),
            P("dp", None),
            P("dp", ("tensor", "probe")),
            P("dp", ("tensor", "probe")),
            P(("tensor", "probe"), "dp"),
            P(),
        ),
        out_specs=(P(None, "dp", ("tensor", "probe")), P(None, "dp")),
        check_vma=False,
    )
```

profile of v0, /device:TPU:8, one launch (start us, length us, event | category | flops | bytes accessed | tf_op | source)
XLA Modules:
  0.0 431.3 jit_solution(1575191020872314107)
XLA Ops:
  7.2 0.7 all-gather.4.cloned.1.call-update
  8.0 0.7 all-gather.6.cloned.1.call-update
  8.7 0.7 all-gather.8.cloned.1.call-update
  9.5 1.3 fusion.49
  14.7 29.7 %multiply_convert_fusion.5 = (bf16[1,4096,896]{1,2,0:T(8,128)(2,1)S(1)}, bf16[1,4096,896]{1,2,0:T(8,128)(2,1)S(1)}, bf16[1,4096,896]{1,2,0:T(8,128)(2,1)S(1)}, bf16[1,4096,896]{1,2,0:T(8,128)(2,1)S(1)}) fusion(s32[]{:T(128)} %bitcast, s32[896]{0:T(1024)S(1)} %get-tuple-element.17, s32[4096]{0:T(1024)S(1)} %iota_multiply_fusion, s32[]{:T(128)} %bitcast.4, ...), kind=kLoop, calls=%fused_computation.15 | loop fusion | flops 286261248 | bytes 29380112 | tf_op jit(solution)/shard_map/convert_element_type | solution.py:23
  44.4 5.0 %fusion.22 = f32[2,128,896]{1,2,0:T(8,128)} fusion(bf16[1,4096,896]{1,2,0:T(8,128)(2,1)S(1)} %get-tuple-element.10, bf16[1,4096,896]{1,2,0:T(8,128)(2,1)S(1)} %get-tuple-element.8, bf16[128,4096]{1,0:T(8,128)(2,1)S(1)} %copy-done), kind=kOutput, calls=%fused_computation.30 | convolution fusion | flops 1886388224 | bytes 16646144 | tf_op jit(solution)/shard_map/tn,pnf->ptf/dot_general | solution.py:56
  49.4 5.0 %fusion.19 = f32[2,128,896]{1,2,0:T(8,128)} fusion(bf16[1,4096,896]{1,2,0:T(8,128)(2,1)S(1)} %get-tuple-element.11, bf16[1,4096,896]{1,2,0:T(8,128)(2,1)S(1)} %get-tuple-element.9, bf16[128,4096]{1,0:T(8,128)(2,1)S(1)} %copy-done), kind=kOutput, calls=%fused_computation.29 | convolution fusion | flops 1886388224 | bytes 16646144 | tf_op jit(solution)/shard_map/tn,pnf->ptf/dot_general | solution.py:56
  54.4 16.8 %multiply_convert_fusion.1 = (bf16[1,896,4096]{1,2,0:T(8,128)(2,1)}, bf16[1,896,4096]{1,2,0:T(8,128)(2,1)}) fusion(s32[]{:T(128)} %bitcast.8, s32[896]{0:T(1024)S(1)} %get-tuple-element.18, s32[]{:T(128)} %bitcast.9), kind=kLoop, calls=%fused_computation.10 | loop fusion | flops 146800640 | bytes 14683656 | tf_op jit(solution)/shard_map/convert_element_type | solution.py:23
  71.2 38.8 %all-gather.4.cloned.1.call-done = bf16[4096,896]{1,0:T(8,128)(2,1)} async-done(((bf16[256,896]{1,0:T(8,128)(2,1)}), bf16[4096,896]{1,0:T(8,128)(2,1)}) %all-gather.4.cloned.1.call-update) | async-done | bytes 7340048 | tf_op jit(solution)/shard_map/all_gather | solution.py:59
  110.0 5.5 %fusion.35 = (f32[128,896]{1,0:T(8,128)}, f32[128,896]{1,0:T(8,128)S(1)}, f32[128,896]{1,0:T(8,128)}, f32[128,896]{1,0:T(8,128)S(1)}, f32[128,896]{1,0:T(8,128)}) fusion(bf16[128,4096]{1,0:T(8,128)(2,1)S(1)} %copy-done, bf16[4096,896]{1,0:T(8,128)(2,1)} %all-gather.4.cloned.1.call-done), kind=kOutput, calls=%fused_computation.44 | convolution fusion | flops 941244416 | bytes 10682368 | tf_op jit(solution)/shard_map/dot_general | solution.py:55
  115.7 0.2 copy.8
  115.9 101.9 %all-gather.6.cloned.1.call-done = bf16[4096,896]{1,0:T(8,128)(2,1)} async-done(((bf16[256,896]{1,0:T(8,128)(2,1)}), bf16[4096,896]{1,0:T(8,128)(2,1)}) %all-gather.6.cloned.1.call-update) | async-done | bytes 7340048 | tf_op jit(solution)/shard_map/all_gather | solution.py:62
  217.9 4.3 %fusion.50 = f32[128,896]{1,0:T(8,128)S(1)} fusion(bf16[128,4096]{1,0:T(8,128)(2,1)S(1)} %copy-done, bf16[4096,896]{1,0:T(8,128)(2,1)} %all-gather.6.cloned.1.call-done), kind=kOutput, calls=%fused_computation.62 | convolution fusion | flops 939524096 | bytes 8847360 | tf_op jit(solution)/shard_map/dot_general | solution.py:55
  222.2 0.2 copy.9
  222.4 121.6 %all-gather.8.cloned.1.call-done = bf16[896,4096]{1,0:T(8,128)(2,1)} async-done(((bf16[896,256]{1,0:T(8,128)(2,1)}), bf16[896,4096]{1,0:T(8,128)(2,1)}) %all-gather.8.cloned.1.call-update) | async-done | bytes 7340048 | tf_op jit(solution)/shard_map/all_gather | solution.py:77
  344.0 6.2 %fusion.10 = f32[2,128,4096]{2,1,0:T(8,128)S(1)} fusion(bf16[896,4096]{1,0:T(8,128)(2,1)} %all-gather.8.cloned.1.call-done, f32[2,128,896]{1,2,0:T(8,128)} %fusion.19, f32[2,128,896]{1,2,0:T(8,128)} %fusion.22, f32[128,896]{0,1:T(8,128)S(1)} %copy.10, f32[128,896]{0,1:T(8,128)S(1)} %copy.9, f32[128,896]{0,1:T(8,128)S(1)} %copy.8), kind=kOutput, calls=%fused_computation.19 | convolution fusion | flops 1880195072 | bytes 14745600 | tf_op jit(solution)/shard_map/ptf,fn->ptn/dot_general | solution.py:81
  350.3 9.5 %fusion.14 = bf16[2,128,4096]{2,1,0:T(8,128)(2,1)} fusion(f32[2,128,4096]{2,1,0:T(8,128)S(1)} %fusion.10, bf16[1,896,4096]{1,2,0:T(8,128)(2,1)} %get-tuple-element.13, bf16[1,896,4096]{1,2,0:T(8,128)(2,1)} %get-tuple-element.12, f32[128,896]{1,0:T(8,128)} %copy-done.3, f32[128,896]{1,0:T(8,128)S(1)} %copy-done.10), kind=kOutput, calls=%fused_computation.23 | convolution fusion | flops 1889173504 | bytes 21889024 | tf_op jit(solution)/shard_map/tf,pfn->ptn/dot_general | solution.py:84
  359.8 1.0 copy.14
  360.8 1.0 copy.15
  361.9 5.3 %fusion.51 = f32[128,896]{0,1:T(8,128)S(1)} fusion(bf16[128,4096]{1,0:T(8,128)(2,1)S(1)} %copy-done.2, bf16[896,4096]{1,0:T(8,128)(2,1)} %all-gather.8.cloned.1.call-done), kind=kOutput, calls=%fused_computation.63 | convolution fusion | flops 939524096 | bytes 8847360 | tf_op jit(solution)/shard_map/tn,fn->tf/dot_general | solution.py:74
  367.2 8.4 %fusion.25 = f32[2,128]{1,0:T(2,128)S(1)} fusion(bf16[1,896,4096]{1,2,0:T(8,128)(2,1)} %get-tuple-element.13, bf16[1,896,4096]{1,2,0:T(8,128)(2,1)} %get-tuple-element.12, bf16[128,4096]{1,0:T(8,128)(2,1)S(1)} %copy-done.2, f32[2,128,896]{1,2,0:T(8,128)S(1)} %copy-done.4, f32[2,128,896]{1,2,0:T(8,128)S(1)} %copy-done.5, f32[128,896]{0,1:T(8,128)S(1)} %copy-done.9, ...), kind=kOutput, calls=%fused_computation.31 | convolution fusion | flops 1889828608 | bytes 20317184 | tf_op jit(solution)/shard_map/tn,pfn->ptf/dot_general | solution.py:75
  375.7 30.0 %psum.7 = f32[2,128]{1,0:T(2,128)S(1)} all-reduce(f32[2,128]{1,0:T(2,128)S(1)} %fusion.25), channel_id=1, replica_groups=mesh['dp'=16,'tensor'=8,'probe'=2] {'tensor','probe'}, use_global_device_ids=true, to_apply=%region_2.0 | all-reduce | flops 256 | bytes 2048 | tf_op jit(solution)/shard_map/psum | solution.py:88
  405.6 0.6 broadcast_multiply_fusion.2
  406.2 18.6 %reduce-scatter.2.cloned.1.call-done = bf16[2,128,256]{2,1,0:T(8,128)(2,1)} async-done(((bf16[2,128,4096]{2,1,0:T(8,128)(2,1)}), bf16[2,128,256]{2,1,0:T(8,128)(2,1)}) %reduce-scatter.2.cloned.1.call-update) | async-done | bytes 131088 | tf_op jit(solution)/shard_map/reduce_scatter | solution.py:89
  (30 shorter events, 0.4 us)
Async XLA Ops:
  7.2 37.2 %copy-start = (bf16[128,4096]{1,0:T(8,128)(2,1)S(1)}, bf16[128,4096]{1,0:T(8,128)(2,1)}, u32[]{:S(2)}) copy-start(bf16[128,4096]{1,0:T(8,128)(2,1)} %param.6) | copy-start | bytes 3145732
  7.2 102.8 %all-gather.4.cloned.1.call-start = ((), (), s32[]{:S(2)}) async-start(), calls=%async_computation.1 | async-start | bytes 7798784 | tf_op jit(solution)/shard_map/all_gather | solution.py:59
  7.9 210.0 %all-gather.6.cloned.1.call-start = ((), (), s32[]{:S(2)}) async-start(), calls=%async_computation.2 | async-start | bytes 7798784 | tf_op jit(solution)/shard_map/all_gather | solution.py:62
  8.7 335.4 %all-gather.8.cloned.1.call-start = ((), (), s32[]{:S(2)}) async-start(), calls=%async_computation.3 | async-start | bytes 7798784 | tf_op jit(solution)/shard_map/all_gather | solution.py:77
  9.4 415.4 %reduce-scatter.2.cloned.1.call-start = ((), (), s32[]{:S(2)}) async-start(), calls=%async_computation.4 | async-start | bytes 2228224 | tf_op jit(solution)/shard_map/reduce_scatter | solution.py:89
  222.2 128.0 %copy-start.3 = (f32[128,896]{1,0:T(8,128)}, f32[128,896]{1,0:T(8,128)S(1)}, u32[]{:S(2)}) copy-start(f32[128,896]{1,0:T(8,128)S(1)} %fusion.50) | copy-start | bytes 1376260
  344.0 6.3 %copy-start.10 = (f32[128,896]{1,0:T(8,128)S(1)}, f32[128,896]{1,0:T(8,128)}, u32[]{:S(2)}) copy-start(f32[128,896]{1,0:T(8,128)} %get-tuple-element.16) | copy-start | bytes 1376260
  350.3 9.5 %copy-start.7 = (f32[128,896]{1,0:T(8,128)S(1)}, f32[128,896]{1,0:T(8,128)}, u32[]{:S(2)}) copy-start(f32[128,896]{1,0:T(8,128)} %get-tuple-element.4) | copy-start | bytes 1376260
  350.3 10.5 %copy-start.6 = (f32[128,896]{1,0:T(8,128)S(1)}, f32[128,896]{1,0:T(8,128)}, u32[]{:S(2)}) copy-start(f32[128,896]{1,0:T(8,128)} %get-tuple-element.6) | copy-start | bytes 1376260
  350.3 11.5 %copy-start.2 = (bf16[128,4096]{1,0:T(8,128)(2,1)S(1)}, bf16[128,4096]{1,0:T(8,128)(2,1)}, u32[]{:S(2)}) copy-start(bf16[128,4096]{1,0:T(8,128)(2,1)} %param.7) | copy-start | bytes 3145732
  361.8 5.3 %copy-start.4 = (f32[2,128,896]{1,2,0:T(8,128)S(1)}, f32[2,128,896]{1,2,0:T(8,128)}, u32[]{:S(2)}) copy-start(f32[2,128,896]{1,2,0:T(8,128)} %fusion.22) | copy-start | bytes 2752516
  361.8 5.3 %copy-start.5 = (f32[2,128,896]{1,2,0:T(8,128)S(1)}, f32[2,128,896]{1,2,0:T(8,128)}, u32[]{:S(2)}) copy-start(f32[2,128,896]{1,2,0:T(8,128)} %fusion.19) | copy-start | bytes 2752516
  361.8 5.3 %copy-start.8 = (f32[128,896]{0,1:T(8,128)S(1)}, f32[128,896]{0,1:T(8,128)}, u32[]{:S(2)}) copy-start(f32[128,896]{0,1:T(8,128)} %copy.14) | copy-start | bytes 1376260
  361.8 5.3 %copy-start.9 = (f32[128,896]{0,1:T(8,128)S(1)}, f32[128,896]{0,1:T(8,128)}, u32[]{:S(2)}) copy-start(f32[128,896]{0,1:T(8,128)} %copy.15) | copy-start | bytes 1376260
  367.2 57.6 %copy-start.1 = (bf16[128,4096]{1,0:T(8,128)(2,1)S(1)}, bf16[128,4096]{1,0:T(8,128)(2,1)}, u32[]{:S(2)}) copy-start(bf16[128,4096]{1,0:T(8,128)(2,1)} %param.6) | copy-start | bytes 3145732
Sparse Core Ops, SparseCore 0:
  10.4 99.5 all-gather.3
  112.4 105.4 all-gather.5
  220.3 123.6 all-gather.7
  360.0 64.7 reduce-scatter.1
where the time goes:
time: 432 us; the launch traced here: 431 us
  waiting for transfers between devices  283 us (66%)
  matrix products  49.4 us (11%)
  other arithmetic  47.1 us (11%)
  blocking collectives  30 us (7%)
  between operations  17.9 us (4%)
    all_gather x1, waiting for transfers between devices, on_device(): piece = lax.all_gather(down_weight, 'dp', axis=1, tiled=True)  122 us
    all_gather x1, waiting for transfers between devices, on_device(): lax.all_gather(up_weight, 'dp', axis=0, tiled=True)  102 us
    convert_element_type x2, other arithmetic, rademacher(): return (signs.astype(jnp.float32) * factor).astype(jnp.bfloat16)  46.5 us
    all_gather x1, waiting for transfers between devices, on_device(): lax.all_gather(gate_weight, 'dp', axis=0, tiled=True)  38.8 us
    psum x1, blocking collectives, on_device(): curvature = lax.psum(local_curv, ('tensor', 'probe')) * out_factor  30 us
    reduce_scatter x1, waiting for transfers between devices, on_device(): lax.psum_scatter(tangent_terms.astype(jnp.bfloat16), ('tensor', 'probe'),...  18.6 us
    dot_general x2, matrix products, project_rows(): jnp.einsum('tn,pnf->ptf', tokens, directions, preferred_element_type=jnp....  9.99 us
    dot_general x2, matrix products, project_rows(): plain = jnp.dot(tokens, weight_piece, preferred_element_type=jnp.float32)  9.89 us
  transfers between devices with their start and end apart: 4, of which 4 were waited for; matrix products, arithmetic and copies ran while one was open for 20% of the time, Pallas kernels for 0%

commit v1 on v0

v1 whole, which is shorter than its diff:
```python
import functools

import jax
import jax.numpy as jnp
import numpy as np
from jax import lax
from jax.experimental import pallas as pl
from jax.experimental.pallas import tpu as pltpu
from jax.sharding import PartitionSpec as P

D = 4096
FF = 14336
UNITS = 224
COLS = 256
BLOCK = 128
MESH = pl.DeviceIdType.MESH
NT = (((1,), (1,)), ((), ()))
BF16, F32, I32 = jnp.bfloat16, jnp.float32, jnp.int32
IN_FACTOR = float(D**-0.5)
OUT_FACTOR = float(FF**-0.5)
OUT_FACTOR_LOW = float(np.asarray(FF**-0.5, np.float32).astype(jnp.bfloat16))
PARTS = ((0, 2 * UNITS), (2 * UNITS, UNITS))


def wrap(value):
    return np.int32((int(value) + 2**31) % 2**32 - 2**31)


STEP = -1640531535


def kernel(
    seeds, tok, cot, wa, out, curv,
    tc, w, dirs, acc, hid, cs, cr, xs, xr, zs, zr, cv, cvc, cvx, cvz,
    loc_sem, a2a_s, a2a_r, ag_s, ag_r, tz_s, tz_r, tx_s, tx_r, tcc_s, tcc_r,
    c_s, c_r, x_s, x_r, z_s, z_r, vc_s, vc_r, vx_s, vx_r, vz_s, vz_r,
):
    dp, tensor, core = lax.axis_index("dp"), lax.axis_index("tensor"), lax.axis_index("probe")
    zh, y = dp // 4, dp % 4
    zl, x = tensor // 4, tensor % 4

    def dev_z(step):
        z = (zh * 2 + zl + step) % 8
        return ((z // 2) * 4 + y, (z % 2) * 4 + x, core)

    def dev_y(step):
        return (zh * 4 + (y + step) % 4, tensor, core)

    def dev_x(step):
        return (dp, zl * 4 + (x + step) % 4, core)

    dev_c = (dp, tensor, 1 - core)

    def remote(src, dst, send, recv, device):
        return pltpu.make_async_remote_copy(
            src_ref=src, dst_ref=dst, send_sem=send, recv_sem=recv,
            device_id=device, device_id_type=MESH,
        )

    barrier = pltpu.get_barrier_semaphore()
    peers = [dev_z(d) for d in range(1, 8)] + [dev_x(d) for d in range(1, 4)] + [dev_y(1), dev_y(3), dev_c]
    for peer in peers:
        pl.semaphore_signal(barrier, inc=1, device_id=peer, device_id_type=MESH)
    pl.semaphore_wait(barrier, len(peers))

    started = []

    def go(copy):
        copy.start()
        started.append(copy)

    def w_at(part, yy, j):
        lo, n = PARTS[part]
        return w.at[yy % 4, (zh + j) % 4, pl.ds(lo, n)]

    def ag_send(part, j):
        lo, n = PARTS[part]
        src = wa.at[zh, pl.ds(lo, n)] if j == 0 else w_at(part, y, j)
        go(remote(src, w_at(part, y, j), ag_s.at[part, j, 0], ag_r.at[part, j, 0], dev_y(1)))
        go(remote(src, w_at(part, y, j), ag_s.at[part, j, 1], ag_r.at[part, j, 1], dev_y(3)))

    def ag_wait(part, j, side, source):
        ref = w_at(part, source, j)
        remote(ref, ref, ag_s.at[part, j, side], ag_r.at[part, j, side], dev_y(1)).wait_recv()

    def ag_relay(part, j):
        side, source, onward = (0, y + 3, 1) if j % 2 == 0 else (1, y + 1, 3)
        ag_wait(part, j, side, source)
        ref = w_at(part, source, j)
        go(remote(ref, ref, ag_s.at[part, j, 2], ag_r.at[part, j, 2], dev_y(onward)))

    def ag_finish(part, j):
        side, source = (1, y + 1) if j % 2 == 0 else (0, y + 3)
        ag_wait(part, j, side, source)
        ag_wait(part, j, 2, y + 2)

    def a2a_send(part, d):
        lo, n = PARTS[part]
        target = (zh + d) % 4
        go(remote(wa.at[target, pl.ds(lo, n)], w_at(part, y, 0), a2a_s.at[part, d - 1], a2a_r.at[part, 3 - d], dev_z(2 * d)))

    def a2a_wait(part, j):
        ref = w_at(part, y, j)
        remote(ref, ref, a2a_s.at[part, j - 1], a2a_r.at[part, j - 1], dev_z(2)).wait_recv()

    def tok_send(d):
        for m, src in enumerate((tok, cot)):
            go(remote(src.at[x, core], tc.at[m, zh, x, core], tz_s.at[m, d - 1], tz_r.at[m, 3 - d], dev_z(2 * d)))

    def tok_forward(j):
        zz = (zh + j) % 4
        for m in range(2):
            ref = tc.at[m, zz, x, core]
            remote(ref, ref, tz_s.at[m, j - 1], tz_r.at[m, j - 1], dev_z(2)).wait_recv()
        ref = tc.at[:, zz, x, core]
        for e in range(1, 4):
            go(remote(ref, ref, tx_s.at[j - 1, e - 1], tx_r.at[j - 1, e - 1], dev_x(e)))

    def tok_share(j):
        zz = (zh + j) % 4
        for e in range(1, 4):
            ref = tc.at[:, zz, (x - e) % 4, core]
            remote(ref, ref, tx_s.at[j - 1, e - 1], tx_r.at[j - 1, e - 1], dev_x(1)).wait_recv()
        ref = tc.at[:, zz, :, core]
        go(remote(ref, ref, tcc_s.at[j - 1], tcc_r.at[j - 1], dev_c))

    def tok_finish(j):
        ref = tc.at[:, (zh + j) % 4, :, 1 - core]
        remote(ref, ref, tcc_s.at[j - 1], tcc_r.at[j - 1], dev_c).wait_recv()

    ag_send(0, 0)
    a2a_send(0, 1)
    a2a_send(0, 3)
    tok_send(1)
    tok_send(3)
    a2a_send(0, 2)
    tok_send(2)
    a2a_send(1, 1)
    a2a_send(1, 3)
    a2a_send(1, 2)
    ag_send(1, 0)
    local = [
        pltpu.make_async_copy(tok, tc.at[0, zh], loc_sem.at[0]),
        pltpu.make_async_copy(cot, tc.at[1, zh], loc_sem.at[1]),
        pltpu.make_async_copy(wa.at[zh], w.at[y, zh], loc_sem.at[2]),
    ]
    for copy in local:
        copy.start()

    first_unit = (tensor * 2 + core) * (4 * UNITS) + zh * UNITS

    def make_signs(m):
        unit_mul, feature_mul = (wrap(STEP), wrap(STEP * FF)) if m < 2 else (wrap(STEP * D), wrap(STEP))
        base = (
            lax.broadcasted_iota(I32, (16, D), 0) * unit_mul + lax.broadcasted_iota(I32, (16, D), 1) * feature_mul
        )

        def body(i, _):
            start = (first_unit + i * 16) * unit_mul + np.int32(40503 * (m + 1))
            for p in range(2):
                u = base + (start + seeds[p])
                u = u ^ lax.shift_right_logical(u, np.int32(16))
                u = u * np.int32(739982445)
                u = u ^ lax.shift_right_logical(u, np.int32(13))
                u = u * np.int32(695872825)
                dirs[2 * m + p, pl.ds(pl.multiple_of(i * 16, 16), 16), :] = jnp.where(u < 0, -1.0, 1.0).astype(BF16)
            return 0

        lax.fori_loop(0, UNITS // 16, body, 0)

    make_signs(0)
    ag_relay(0, 0)
    make_signs(1)
    ag_relay(1, 0)
    for j in (1, 3):
        a2a_wait(0, j)
        ag_send(0, j)
    make_signs(2)
    for j in (1, 3):
        tok_forward(j)
    for j in (1, 3):
        ag_relay(0, j)
    a2a_wait(0, 2)
    ag_send(0, 2)
    tok_forward(2)
    for j in (1, 3):
        a2a_wait(1, j)
        ag_send(1, j)
    for j in (1, 3):
        tok_share(j)
    ag_relay(0, 2)
    a2a_wait(1, 2)
    ag_send(1, 2)
    tok_share(2)
    for j in (1, 3, 2):
        tok_finish(j)
    for copy in local:
        copy.wait()
    for j in (1, 3):
        ag_relay(1, j)

    def rows_of(m, lo, n):
        return tc[m, pl.ds(lo, n)].reshape(n * BLOCK, D)

    def dir_body(i, _):
        acc[i] = lax.dot_general(rows_of(i // 4, 0, 4), dirs[i], NT, preferred_element_type=F32)
        return 0

    lax.fori_loop(0, 6, dir_body, 0)
    ag_relay(1, 2)
    for j in (0, 1, 3, 2):
        ag_finish(0, j)

    def gate_rows(i):
        return w[:, :, pl.ds(i * UNITS, UNITS), :]

    def plain(i):
        def body(b, total):
            yy, zz = b // 4, b % 4
            col = pl.ds(pl.multiple_of((zz * 4 + yy) * COLS, COLS), COLS)
            lhs = tc[i // 2, :, :, :, :, col].reshape(4 * BLOCK, COLS)
            return total + lax.dot_general(
                lhs, w[yy, zz, pl.ds(i * UNITS, UNITS), :], NT, preferred_element_type=F32
            )

        acc[6 + i] = lax.fori_loop(0, 16, body, jnp.zeros((4 * BLOCK, UNITS), F32))

    plain(0)
    plain(1)

    def point(i, _):
        r = pl.ds(pl.multiple_of(i * 32, 32), 32)
        gate, up = acc[6, r, :], acc[7, r, :]
        s = jax.nn.sigmoid(gate)
        silu = gate * s
        slope = s * (1.0 + gate * (1.0 - s))
        bend = s * (1.0 - s) * (2.0 + gate * (1.0 - 2.0 * s))
        hid[2, r, :] = (silu * up).astype(BF16)
        for p in range(2):
            gd, ud = acc[p, r, :] * IN_FACTOR, acc[2 + p, r, :] * IN_FACTOR
            hd = slope * gd * up + silu * ud
            hid[p, r, :] = hd.astype(BF16)
            acc[2 + p, r, :] = hd
            acc[p, r, :] = bend * gd * gd * up + 2.0 * slope * gd * ud
        return 0

    lax.fori_loop(0, 16, point, 0)
    for j in (0, 1, 3, 2):
        ag_finish(1, j)
    plain(2)

    cv[0] = jnp.zeros((8, 4 * BLOCK), F32)
    for p in range(2):
        terms = acc[8] * acc[p] + (2.0 * OUT_FACTOR_LOW) * acc[4 + p] * acc[2 + p]
        cv[0, pl.ds(p, 1), :] = jnp.sum(terms.T, axis=0, keepdims=True) * OUT_FACTOR
    go(remote(cv.at[0], cvc, vc_s.at[0], vc_r.at[0], dev_c))

    def columns(e, lr, other):
        return (((zl + lr) % 2) * 4 + (x + e) % 4) * 2 + other

    def tangent(p, b):
        col = pl.ds(pl.multiple_of(b * COLS, COLS), COLS)
        one = jnp.dot(hid[p], w[b % 4, b // 4, pl.ds(2 * UNITS, UNITS), :], preferred_element_type=F32)
        two = jnp.dot(hid[2], dirs[4 + p, :, col], preferred_element_type=F32)
        return one + two * OUT_FACTOR_LOW

    ORDER = (2, 1, 3, 0)

    def give(e, lr):
        k = e * 2 + lr
        return remote(cs.at[k], cr.at[k], c_s.at[k], c_r.at[k], dev_c)

    def x_copy(e, lr):
        return remote(xs.at[e, lr], xr.at[e - 1, lr], x_s.at[e - 1, lr], x_r.at[e - 1, lr], dev_x(e))

    for e in ORDER:

        def body(lr, _, e=e):
            def probe(p, _):
                cs[e * 2 + lr, p] = tangent(p, columns(e, lr, 1 - core)).astype(BF16)
                return 0

            lax.fori_loop(0, 2, probe, 0)
            give(e, lr).start()

            def probe2(p, _):
                xs[e, lr, p] = tangent(p, columns(e, lr, core)).astype(BF16)
                return 0

            lax.fori_loop(0, 2, probe2, 0)
            give(e, lr).wait_recv()

            def merge(i, _):
                r = pl.ds(pl.multiple_of(i * 64, 64), 64)
                for p in range(2):
                    xs[e, lr, p, r, :] = (
                        xs[e, lr, p, r, :].astype(F32) + cr[e * 2 + lr, p, r, :].astype(F32)
                    ).astype(BF16)
                return 0

            lax.fori_loop(0, 8, merge, 0)
            if e:
                x_copy(e, lr).start()
            return 0

        lax.fori_loop(0, 2, body, 0)
        if e == 1:
            ref = cvc
            remote(ref, ref, vc_s.at[0], vc_r.at[0], dev_c).wait_recv()
            cv[1] = cv[0] + cvc[...]
            for d in range(1, 4):
                go(remote(cv.at[1], cvx.at[d - 1], vx_s.at[d - 1], vx_r.at[d - 1], dev_x(d)))
        if e == 0:
            for d in range(1, 4):
                remote(cv.at[1], cvx.at[d - 1], vx_s.at[d - 1], vx_r.at[d - 1], dev_x(d)).wait_recv()
            cv[2] = (cv[1] + cvx[0]) + (cvx[1] + cvx[2])
            for d in range(1, 8):
                zz = ((zh * 2 + zl + d) % 8) // 2
                src = cv.at[2, :, pl.ds(pl.multiple_of(zz * BLOCK, BLOCK), BLOCK)]
                go(remote(src, cvz.at[d - 1], vz_s.at[d - 1], vz_r.at[d - 1], dev_z(d)))

    def z_copy(d, lr):
        zz = ((zh * 2 + zl + d) % 8) // 2
        return remote(
            zs.at[lr, :, pl.ds(pl.multiple_of(zz * BLOCK, BLOCK), BLOCK)], zr.at[d - 1], z_s.at[d - 1], z_r.at[d - 1], dev_z(d)
        )

    for lr, steps in ((1, (1, 7, 3, 5)), (0, (2, 6, 4))):
        for e in (1, 3, 2):
            x_copy(e, lr).wait_recv()

        def merge(i, _, lr=lr):
            r = pl.ds(pl.multiple_of(i * 64, 64), 64)
            for p in range(2):
                total = xs[0, lr, p, r, :].astype(F32)
                for e in range(3):
                    total = total + xr[e, lr, p, r, :].astype(F32)
                zs[lr, p, r, :] = total.astype(BF16)
            return 0

        lax.fori_loop(0, 8, merge, 0)
        for d in steps:
            go(z_copy(d, lr))

    for d in range(1, 8):
        remote(cvz.at[d - 1], cvz.at[d - 1], vz_s.at[d - 1], vz_r.at[d - 1], dev_z(d)).wait_recv()
    total = cv[2, :, pl.ds(pl.multiple_of(zh * BLOCK, BLOCK), BLOCK)]
    for d in range(7):
        total = total + cvz[d]
    curv[...] = total[:2]

    for d in range(1, 8):
        remote(zr.at[d - 1], zr.at[d - 1], z_s.at[d - 1], z_r.at[d - 1], dev_z(d)).wait_recv()

    def last(i, _):
        r = pl.ds(pl.multiple_of(i * 32, 32), 32)
        own = pl.ds(pl.multiple_of(zh * BLOCK + i * 32, 32), 32)
        for p in range(2):
            total = zs[0, p, own, :].astype(F32)
            for d in range(7):
                total = total + zr[d, p, r, :].astype(F32)
            out[p, r, :] = total.astype(BF16)
        return 0

    lax.fori_loop(0, 4, last, 0)
    for copy in started:
        copy.wait_send()
    for e in ORDER:
        for lr in range(2):
            give(e, lr).wait_send()
            if e:
                x_copy(e, lr).wait_send()


def on_device(tokens, cotangent, gate_weight, up_weight, down_weight, probe_seeds):
    weights = jnp.concatenate(
        [part.reshape(4, UNITS, COLS) for part in (gate_weight.T, up_weight.T, down_weight)], axis=1
    )
    dma = pltpu.SemaphoreType.DMA
    vmem = pltpu.VMEM
    hbm = pl.BlockSpec(memory_space=pl.ANY)
    tangent, curvature = pl.pallas_call(
        kernel,
        out_shape=(
            jax.ShapeDtypeStruct((2, BLOCK, COLS), BF16),
            jax.ShapeDtypeStruct((2, BLOCK), F32),
        ),
        in_specs=[pl.BlockSpec(memory_space=pltpu.SMEM), hbm, hbm, hbm],
        out_specs=(pl.BlockSpec(memory_space=pltpu.VMEM), pl.BlockSpec(memory_space=pltpu.VMEM)),
        scratch_shapes=[
            vmem((2, 4, 4, 2, 16, D), BF16),
            vmem((4, 4, 3 * UNITS, COLS), BF16),
            vmem((6, UNITS, D), BF16),
            vmem((9, 4 * BLOCK, UNITS), F32),
            vmem((3, 4 * BLOCK, UNITS), BF16),
            vmem((8, 2, 4 * BLOCK, COLS), BF16),
            vmem((8, 2, 4 * BLOCK, COLS), BF16),
            vmem((4, 2, 2, 4 * BLOCK, COLS), BF16),
            vmem((3, 2, 2, 4 * BLOCK, COLS), BF16),
            vmem((2, 2, 4 * BLOCK, COLS), BF16),
            vmem((7, 2, BLOCK, COLS), BF16),
            vmem((3, 8, 4 * BLOCK), F32),
            vmem((8, 4 * BLOCK), F32),
            vmem((3, 8, 4 * BLOCK), F32),
            vmem((7, 8, BLOCK), F32),
            dma((3,)),
            dma((2, 3)), dma((2, 3)),
            dma((2, 4, 3)), dma((2, 4, 3)),
            dma((2, 3)), dma((2, 3)),
            dma((3, 3)), dma((3, 3)),
            dma((3,)), dma((3,)),
            dma((8,)), dma((8,)),
            dma((3, 2)), dma((3, 2)),
            dma((7,)), dma((7,)),
            dma((1,)), dma((1,)),
            dma((3,)), dma((3,)),
            dma((7,)), dma((7,)),
        ],
        name="curvature_probes",
        cost_estimate=pl.CostEstimate(flops=13 * 2 * 512 * D * UNITS, bytes_accessed=4 * 2**20, transcendentals=512 * UNITS),
        compiler_params=pltpu.CompilerParams(
            collective_id=0, has_side_effects=True, vmem_limit_bytes=60 * 2**20
        ),
    )(
        probe_seeds,
        tokens.reshape(4, 2, 16, D),
        cotangent.reshape(4, 2, 16, D),
        weights,
    )
    return tangent, curvature


def solution(mesh):
    return jax.shard_map(
        on_device,
        mesh=mesh,
        in_specs=(
            P("dp", None),
            P("dp", None),
            P("dp", ("tensor", "probe")),
            P("dp", ("tensor", "probe")),
            P(("tensor", "probe"), "dp"),
            P(),
        ),
        out_specs=(P(None, "dp", ("tensor", "probe")), P(None, "dp")),
        check_vma=False,
    )
```

time: 432 us -> 183 us (0.42)
  waiting for transfers between devices: 283 us -> 0 us
  Pallas kernels: 0 us -> 175 us
  matrix products: 49.4 us -> 0 us
  other arithmetic: 47.1 us -> 1.18 us
  blocking collectives: 30 us -> 0 us
  between operations: 17.9 us -> 0.66 us
    all_gather x3 -> x0, waiting for transfers between devices: 262 us -> none  [the longest x1 122 us: on_device(): piece = lax.all_gather(down_weight, 'dp', axis=1, tiled=True)]
    pallas_call x0 -> x1, Pallas kernels: none -> 175 us  [on_device(): pl.pallas_call(kernel, out_shape=(jax.ShapeDtypeStruct((2, BLOCK, COLS),...]
    dot_general x8 -> x0, matrix products: 49.4 us -> none  [the longest x2 9.99 us: project_rows(): jnp.einsum('tn,pnf->ptf', tokens, directions, preferred_element_type=jnp....]
    convert_element_type x2 -> x0, other arithmetic: 46.5 us -> none  [rademacher(): return (signs.astype(jnp.float32) * factor).astype(jnp.bfloat16)]
    psum x1 -> x0, blocking collectives: 30 us -> none  [on_device(): curvature = lax.psum(local_curv, ('tensor', 'probe')) * out_factor]
    reduce_scatter x1 -> x0, waiting for transfers between devices: 18.6 us -> none  [on_device(): lax.psum_scatter(tangent_terms.astype(jnp.bfloat16), ('tensor', 'probe'),...]
  transfers between devices with their start and end apart: 4 -> 0, of which waited for: 4 -> 0; matrix products, arithmetic and copies ran while one was open for 20% -> 0% of each run, Pallas kernels for 0% -> 0%
where the time goes in v1:
time: 183 us; the launch traced here: 182 us
  Pallas kernels  175 us (96%)
  local copies, waits for them, and re-layouts  5.23 us (3%)
    pallas_call x1, Pallas kernels, on_device(): pl.pallas_call(kernel, out_shape=(jax.ShapeDtypeStruct((2, BLOCK, COLS),...  175 us

profile of v1, /device:TPU:8, one launch (start us, length us, event | category | flops | bytes accessed | tf_op | source)
XLA Modules:
  0.0 181.9 jit_solution(17538980794409734165)
XLA Ops:
  0.6 0.0 copy-start
  0.6 1.3 copy.8
  1.9 1.2 copy.9
  3.1 0.0 copy-done
  3.2 1.2 pad_maximum_fusion.wa
  4.3 174.9 %curvature_probes.1 = (bf16[2,128,256]{2,1,0:T(8,128)(2,1)}, f32[2,128]{1,0:T(2,128)}) custom-call(s32[2]{0:T(128)} %seeds.1, bf16[4,2,16,4096]{3,2,1,0:T(8,128)(2,1)} %bitcast.12, bf16[4,2,16,4096]{3,2,1,0:T(8,128)(2,1)} %bitcast.13, bf16[4,672,256]{2,1,0:T(8,128)(2,1)} %pad_maximum_fusion.wa), custom_call_target="tpu_custom_call" | custom-call | flops 12213813248 | bytes 4194304 | tf_op jit(solution)/shard_map/curvature_probes/pallas_call | solution.py:382
  179.2 1.6 copy.12
  180.8 1.2 copy.13
Async XLA Ops:
  0.6 2.5 %copy-start = (bf16[896,256]{1,0:T(8,128)(2,1)S(1)}, bf16[896,256]{1,0:T(8,128)(2,1)}, u32[]{:S(2)}) copy-start(bf16[896,256]{1,0:T(8,128)(2,1)} %param.10) | copy-start | bytes 1376260

commit v2 on v1

v2 whole, which is shorter than its diff:
```python
import functools

import jax
import jax.numpy as jnp
import numpy as np
from jax import lax
from jax.experimental import pallas as pl
from jax.experimental.pallas import tpu as pltpu
from jax.sharding import PartitionSpec as P

D = 4096
FF = 14336
UNITS = 224
COLS = 256
BLOCK = 128
MESH = pl.DeviceIdType.MESH
NT = (((1,), (1,)), ((), ()))
BF16, F32, I32 = jnp.bfloat16, jnp.float32, jnp.int32
IN_FACTOR = float(D**-0.5)
OUT_FACTOR = float(FF**-0.5)
OUT_FACTOR_LOW = float(np.asarray(FF**-0.5, np.float32).astype(jnp.bfloat16))
PARTS = ((0, 2 * UNITS), (2 * UNITS, UNITS))


def wrap(value):
    return np.int32((int(value) + 2**31) % 2**32 - 2**31)


STEP = -1640531535


def kernel(
    seeds, tok, cot, wa, out, curv,
    tc, w, dirs, acc, hid, cs0, cr0, s0, xr0, zr0, cs1, cr1, s1, zr1, xr1, cv, cvc, cvx, cvz,
    loc_sem, a2a_s, a2a_r, ag_s, ag_r, tz_s, tz_r, tx_s, tx_r, tcc_s, tcc_r,
    c_s, c_r, x0_s, x0_r, z0_s, z0_r, z1_s, z1_r, x1_s, x1_r, vc_s, vc_r, vx_s, vx_r, vz_s, vz_r,
):
    dp, tensor, core = lax.axis_index("dp"), lax.axis_index("tensor"), lax.axis_index("probe")
    zh, y = dp // 4, dp % 4
    zl, x = tensor // 4, tensor % 4

    def dev_z(step):
        z = (zh * 2 + zl + step) % 8
        return ((z // 2) * 4 + y, (z % 2) * 4 + x, core)

    def dev_y(step):
        return (zh * 4 + (y + step) % 4, tensor, core)

    def dev_x(step):
        return (dp, zl * 4 + (x + step) % 4, core)

    dev_c = (dp, tensor, 1 - core)

    def remote(src, dst, send, recv, device):
        return pltpu.make_async_remote_copy(
            src_ref=src, dst_ref=dst, send_sem=send, recv_sem=recv,
            device_id=device, device_id_type=MESH,
        )

    barrier = pltpu.get_barrier_semaphore()
    peers = [dev_z(d) for d in range(1, 8)] + [dev_x(d) for d in range(1, 4)] + [dev_y(1), dev_y(3), dev_c]
    for peer in peers:
        pl.semaphore_signal(barrier, inc=1, device_id=peer, device_id_type=MESH)
    pl.semaphore_wait(barrier, len(peers))

    started = []

    def go(copy):
        copy.start()
        started.append(copy)

    def w_at(part, yy, j):
        lo, n = PARTS[part]
        return w.at[yy % 4, (zh + j) % 4, pl.ds(lo, n)]

    def ag_send(part, j):
        lo, n = PARTS[part]
        src = wa.at[zh, pl.ds(lo, n)] if j == 0 else w_at(part, y, j)
        go(remote(src, w_at(part, y, j), ag_s.at[part, j, 0], ag_r.at[part, j, 0], dev_y(1)))
        go(remote(src, w_at(part, y, j), ag_s.at[part, j, 1], ag_r.at[part, j, 1], dev_y(3)))

    def ag_wait(part, j, side, source):
        ref = w_at(part, source, j)
        remote(ref, ref, ag_s.at[part, j, side], ag_r.at[part, j, side], dev_y(1)).wait_recv()

    def ag_relay(part, j):
        side, source, onward = (0, y + 3, 1) if j % 2 == 0 else (1, y + 1, 3)
        ag_wait(part, j, side, source)
        ref = w_at(part, source, j)
        go(remote(ref, ref, ag_s.at[part, j, 2], ag_r.at[part, j, 2], dev_y(onward)))

    def ag_finish(part, j):
        side, source = (1, y + 1) if j % 2 == 0 else (0, y + 3)
        ag_wait(part, j, side, source)
        ag_wait(part, j, 2, y + 2)

    def a2a_send(part, d):
        lo, n = PARTS[part]
        target = (zh + d) % 4
        go(remote(wa.at[target, pl.ds(lo, n)], w_at(part, y, 0), a2a_s.at[part, d - 1], a2a_r.at[part, 3 - d], dev_z(2 * d)))

    def a2a_wait(part, j):
        ref = w_at(part, y, j)
        remote(ref, ref, a2a_s.at[part, j - 1], a2a_r.at[part, j - 1], dev_z(2)).wait_recv()

    def tz(up, k, block, m, own=False):
        src = (tok, cot)[m].at[x, core] if own else tc.at[m, block % 4, x, core]
        side = 0 if up else 1
        return remote(src, tc.at[m, block % 4, x, core], tz_s.at[side, k], tz_r.at[side, k], dev_z(1 if up else 7))

    def tz_block(up, k):
        near = zh + 3 if up else zh + 1
        return (near, (0, 1, 0)[k] if up else (1, 0, 1)[k]) if k < 2 else (zh + 2, 0 if up else 1)

    def tz_wait(up, k):
        block, m = tz_block(up, k)
        tz(up, k, block, m).wait_recv()

    def tz_open(up):
        for k in range(2):
            m = k if up else 1 - k

            @pl.when(zl == (1 if up else 0))
            def _():
                tz(up, k, zh, m, own=True).start()

    def tz_pass(up, k):
        block, m = tz_block(up, k)

        @pl.when(zl == (0 if up else 1))
        def _():
            tz_wait(up, k)
            tz(up, k, block, m).start()

    def tz_half(up):
        @pl.when(zl == (1 if up else 0))
        def _():
            tz_wait(up, 0)
            tz(up, 2, zh + 3 if up else zh + 1, 0 if up else 1).start()

    def tz_rest(up, k):
        if k == 0:
            return

        @pl.when(zl == (1 if up else 0))
        def _():
            tz_wait(up, k)

    def tx(j, side):
        ref = tc.at[:, (zh + j) % 4, x, core]
        return remote(ref, ref, tx_s.at[j - 1, side], tx_r.at[j - 1, side], dev_x(1 if side == 0 else 3))

    def tx_send(j):
        go(tx(j, 0))
        go(tx(j, 1))

    def tx_relay(j):
        for side in range(2):
            ref = tc.at[:, (zh + j) % 4, (x + (3 if side == 0 else 1)) % 4, core]
            remote(ref, ref, tx_s.at[j - 1, side], tx_r.at[j - 1, side], dev_x(1)).wait_recv()
            ref = ref.at[side]
            go(remote(ref, ref, tx_s.at[j - 1, 2 + side], tx_r.at[j - 1, 2 + side], dev_x(1 if side == 0 else 3)))

    def tok_share(j):
        for side in range(2):
            ref = tc.at[side, (zh + j) % 4, (x + 2) % 4, core]
            remote(ref, ref, tx_s.at[j - 1, 2 + side], tx_r.at[j - 1, 2 + side], dev_x(1)).wait_recv()
        ref = tc.at[:, (zh + j) % 4, :, core]
        go(remote(ref, ref, tcc_s.at[j - 1], tcc_r.at[j - 1], dev_c))

    def tok_finish(j):
        ref = tc.at[:, (zh + j) % 4, :, 1 - core]
        remote(ref, ref, tcc_s.at[j - 1], tcc_r.at[j - 1], dev_c).wait_recv()

    tz_open(True)
    tz_open(False)
    ag_send(0, 0)
    local = [
        pltpu.make_async_copy(tok, tc.at[0, zh], loc_sem.at[0]),
        pltpu.make_async_copy(cot, tc.at[1, zh], loc_sem.at[1]),
        pltpu.make_async_copy(wa.at[zh], w.at[y, zh], loc_sem.at[2]),
    ]
    for copy in local:
        copy.start()

    first_unit = (tensor * 2 + core) * (4 * UNITS) + zh * UNITS

    def make_signs(m, lo, hi):
        unit_mul, feature_mul = (wrap(STEP), wrap(STEP * FF)) if m < 2 else (wrap(STEP * D), wrap(STEP))
        base = (
            lax.broadcasted_iota(I32, (16, D), 0) * unit_mul + lax.broadcasted_iota(I32, (16, D), 1) * feature_mul
        )

        def body(i, _):
            start = (first_unit + i * 16) * unit_mul + np.int32(40503 * (m + 1))
            for p in range(2):
                u = base + (start + seeds[p])
                u = u ^ lax.shift_right_logical(u, np.int32(16))
                u = u * np.int32(739982445)
                u = u ^ lax.shift_right_logical(u, np.int32(13))
                u = u * np.int32(695872825)
                dirs[2 * m + p, pl.ds(pl.multiple_of(i * 16, 16), 16), :] = jnp.where(u < 0, -1.0, 1.0).astype(BF16)
            return 0

        lax.fori_loop(lo, hi, body, 0)

    make_signs(0, 0, 7)
    for k in range(2):
        for up in (True, False):
            tz_pass(up, k)
        make_signs(0, 7 + 3 * k, 10 + 4 * k)
    for up in (True, False):
        tz_half(up)
    a2a_send(0, 1)
    a2a_send(0, 3)
    ag_relay(0, 0)
    ag_send(1, 0)
    make_signs(1, 0, 4)
    for up in (True, False):
        tz_rest(up, 1)
    tx_send(1)
    tx_send(3)
    make_signs(1, 4, 8)
    for up in (True, False):
        tz_pass(up, 2)
    make_signs(1, 8, 14)
    for up in (True, False):
        tz_rest(up, 2)
    tx_send(2)
    make_signs(2, 0, 3)
    for j in (1, 3):
        a2a_wait(0, j)
        ag_send(0, j)
    a2a_send(0, 2)
    ag_relay(1, 0)
    tx_relay(1)
    tx_relay(3)
    make_signs(2, 3, 14)
    tx_relay(2)
    for j in (1, 3):
        tok_share(j)
    a2a_wait(0, 2)
    ag_send(0, 2)
    for d in (1, 3, 2):
        a2a_send(1, d)
    for j in (1, 3):
        ag_relay(0, j)
    tok_share(2)
    for j in (1, 3, 2):
        tok_finish(j)
    for copy in local:
        copy.wait()

    def rows_of(m, lo, n):
        return tc[m, pl.ds(lo, n)].reshape(n * BLOCK, D)

    def dir_body(i, _):
        acc[i] = lax.dot_general(rows_of(i // 4, 0, 4), dirs[i], NT, preferred_element_type=F32)
        return 0

    lax.fori_loop(0, 3, dir_body, 0)
    for j in (1, 3):
        a2a_wait(1, j)
        ag_send(1, j)
    ag_relay(0, 2)
    lax.fori_loop(3, 6, dir_body, 0)
    a2a_wait(1, 2)
    ag_send(1, 2)
    for j in (0, 1, 3, 2):
        ag_finish(0, j)
    for j in (1, 3):
        ag_relay(1, j)

    def plain(i, _):
        rhs = jnp.concatenate([w[b % 4, b // 4, pl.ds(i * UNITS, UNITS), :] for b in range(16)], axis=1)
        acc[6 + i] = lax.dot_general(rows_of(i // 2, 0, 4), rhs, NT, preferred_element_type=F32)
        return 0

    lax.fori_loop(0, 2, plain, 0)
    ag_relay(1, 2)

    def point(i, _):
        r = pl.ds(pl.multiple_of(i * 32, 32), 32)
        gate, up = acc[6, r, :], acc[7, r, :]
        s = jax.nn.sigmoid(gate)
        silu = gate * s
        slope = s * (1.0 + gate * (1.0 - s))
        bend = s * (1.0 - s) * (2.0 + gate * (1.0 - 2.0 * s))
        hid[2, r, :] = (silu * up).astype(BF16)
        for p in range(2):
            gd, ud = acc[p, r, :] * IN_FACTOR, acc[2 + p, r, :] * IN_FACTOR
            hd = slope * gd * up + silu * ud
            hid[p, r, :] = hd.astype(BF16)
            acc[2 + p, r, :] = hd
            acc[p, r, :] = bend * gd * gd * up + 2.0 * slope * gd * ud
        return 0

    lax.fori_loop(0, 16, point, 0)
    for j in (0, 1, 3, 2):
        ag_finish(1, j)
    lax.fori_loop(2, 3, plain, 0)

    cv[0] = jnp.zeros((8, 4 * BLOCK), F32)
    for p in range(2):
        terms = acc[8] * acc[p] + (2.0 * OUT_FACTOR_LOW) * acc[4 + p] * acc[2 + p]
        cv[0, pl.ds(p, 1), :] = jnp.sum(terms.T, axis=0, keepdims=True) * OUT_FACTOR
    go(remote(cv.at[0], cvc, vc_s.at[0], vc_r.at[0], dev_c))

    def columns(e, lr, other):
        return (((zl + lr) % 2) * 4 + (x + e) % 4) * 2 + other

    def tangent(p, b):
        col = pl.ds(pl.multiple_of(b * COLS, COLS), COLS)
        one = jnp.dot(hid[p], w[b % 4, b // 4, pl.ds(2 * UNITS, UNITS), :], preferred_element_type=F32)
        two = jnp.dot(hid[2], dirs[4 + p, :, col], preferred_element_type=F32)
        return one + two * OUT_FACTOR_LOW

    def group(p, g):
        n, mine, out_ref, in_ref = (4, s1, cs1, cr1) if p else (2, s0, cs0, cr0)

        def column(i, side):
            return columns((i - x) % 4, g, side) if p else columns(g, i, side)

        def theirs(i, _):
            out_ref[g, pl.ds(i, 1)] = tangent(p, column(i, 1 - core)).astype(BF16)[None]
            return 0

        lax.fori_loop(0, n, theirs, 0)
        give = remote(out_ref.at[g], in_ref.at[g], c_s.at[p, g], c_r.at[p, g], dev_c)
        go(give)

        def ours(i, _):
            mine[g, pl.ds(i, 1)] = tangent(p, column(i, core)).astype(BF16)[None]
            return 0

        lax.fori_loop(0, n, ours, 0)
        give.wait_recv()

        def merge(i, _):
            r = pl.ds(pl.multiple_of((i % 8) * 64, 64), 64)
            mine[g, i // 8, r, :] = (mine[g, i // 8, r, :].astype(F32) + in_ref[g, i // 8, r, :].astype(F32)).astype(BF16)
            return 0

        lax.fori_loop(0, 8 * n, merge, 0)

    def z_rows(d, u):
        return pl.ds(pl.multiple_of((((zh * 2 + zl + d) % 8) // 2) * BLOCK + u * 64, 64), 64)

    def z_part(up, u, d):
        far = d if up else 8 - d
        return s1.at[far % 2, :, z_rows(far, u)]

    def z_hop(up, u, d):
        side = 0 if up else 1
        return remote(
            z_part(up, u, d), zr1.at[side, u, d - 1], z1_s.at[side, u, d - 1], z1_r.at[side, u, d - 1], dev_z(1 if up else 7)
        )

    def z_add(up, u, d):
        z_hop(up, u, d).wait_recv()
        far = (d - 1 if up else 9 - d) % 8

        def body(i, _):
            r = z_rows(far, u)
            s1[far % 2, i, r, :] = (
                s1[far % 2, i, r, :].astype(F32) + zr1[0 if up else 1, u, d - 1, i].astype(F32)
            ).astype(BF16)
            return 0

        lax.fori_loop(0, 4, body, 0)

    def z_step(d):
        for up in (True, False):
            lane = 0 if up else 1
            z_add(up, lane, d + 1)
            go(z_hop(up, lane, d))
        if d > 1:
            for up in (True, False):
                lane = 1 if up else 0
                z_add(up, lane, d)
                go(z_hop(up, lane, d - 1))

    def x_hop(up, u, d):
        side = 0 if up else 1
        e = d if up else 4 - d
        return remote(s0.at[e, u], xr0.at[side, u, d - 1], x0_s.at[side, u, d - 1], x0_r.at[side, u, d - 1], dev_x(1 if up else 3))

    def x_add(up, u, d):
        x_hop(up, u, d).wait_recv()
        e = (d - 1 if up else 5 - d) % 4

        def body(i, _):
            r = pl.ds(pl.multiple_of(i * 64, 64), 64)
            s0[e, u, r, :] = (s0[e, u, r, :].astype(F32) + xr0[0 if up else 1, u, d - 1, r, :].astype(F32)).astype(BF16)
            return 0

        lax.fori_loop(0, 8, body, 0)

    group(1, 0)
    go(z_hop(True, 0, 4))
    go(z_hop(False, 1, 4))
    group(1, 1)
    go(z_hop(True, 1, 3))
    go(z_hop(False, 0, 3))
    group(0, 2)
    go(x_hop(True, 0, 2))
    go(x_hop(False, 1, 2))
    z_step(3)
    group(0, 1)
    go(x_hop(True, 1, 1))
    group(0, 3)
    go(x_hop(False, 0, 1))
    x_add(True, 0, 2)
    go(x_hop(True, 0, 1))
    x_add(False, 1, 2)
    go(x_hop(False, 1, 1))
    remote(cvc, cvc, vc_s.at[0], vc_r.at[0], dev_c).wait_recv()
    cv[1] = cv[0] + cvc[...]
    for d in range(1, 4):
        go(remote(cv.at[1], cvx.at[d - 1], vx_s.at[d - 1], vx_r.at[d - 1], dev_x(d)))
    z_step(2)
    group(0, 0)
    for d in range(1, 4):
        remote(cv.at[1], cvx.at[d - 1], vx_s.at[d - 1], vx_r.at[d - 1], dev_x(d)).wait_recv()
    cv[2] = (cv[1] + cvx[0]) + (cvx[1] + cvx[2])
    for d in range(1, 8):
        zz = ((zh * 2 + zl + d) % 8) // 2
        src = cv.at[2, :, pl.ds(pl.multiple_of(zz * BLOCK, BLOCK), BLOCK)]
        go(remote(src, cvz.at[d - 1], vz_s.at[d - 1], vz_r.at[d - 1], dev_z(d)))
    z_step(1)

    def z_copy(d):
        zz = ((zh * 2 + zl + d) % 8) // 2
        return remote(
            s0.at[0, d % 2, pl.ds(pl.multiple_of(zz * BLOCK, BLOCK), BLOCK)], zr0.at[d - 1], z0_s.at[d - 1], z0_r.at[d - 1], dev_z(d)
        )

    for lr, steps in ((1, (1, 7, 3, 5)), (0, (2, 6, 4))):
        x_add(True, lr, 1)
        x_add(False, lr, 1)
        for d in steps:
            go(z_copy(d))

    def x_copy(e):
        return remote(
            s1.at[0, (x + e) % 4, pl.ds(pl.multiple_of(zh * BLOCK, BLOCK), BLOCK)], xr1.at[e - 1], x1_s.at[e - 1], x1_r.at[e - 1], dev_x(e)
        )

    for up in (True, False):
        for u in range(2):
            z_add(up, u, 1)
    for e in range(1, 4):
        go(x_copy(e))

    for d in range(1, 8):
        remote(cvz.at[d - 1], cvz.at[d - 1], vz_s.at[d - 1], vz_r.at[d - 1], dev_z(d)).wait_recv()
    total = cv[2, :, pl.ds(pl.multiple_of(zh * BLOCK, BLOCK), BLOCK)]
    for d in range(7):
        total = total + cvz[d]
    curv[...] = total[:2]

    for d in range(1, 8):
        z_copy(d).wait_recv()
    for e in range(1, 4):
        x_copy(e).wait_recv()

    def last(i, _):
        r = pl.ds(pl.multiple_of(i * 32, 32), 32)
        own = pl.ds(pl.multiple_of(zh * BLOCK + i * 32, 32), 32)
        total = s0[0, 0, own, :].astype(F32)
        for d in range(7):
            total = total + zr0[d, r, :].astype(F32)
        out[0, r, :] = total.astype(BF16)
        total = s1[0, x, own, :].astype(F32)
        for e in range(3):
            total = total + xr1[e, r, :].astype(F32)
        out[1, r, :] = total.astype(BF16)
        return 0

    lax.fori_loop(0, 4, last, 0)
    for up in (True, False):
        for k in range(3):
            block, m = tz_block(up, k)
            tz(up, k, block, m).wait_send()
    for copy in started:
        copy.wait_send()


def on_device(tokens, cotangent, gate_weight, up_weight, down_weight, probe_seeds):
    weights = jnp.concatenate(
        [part.reshape(4, UNITS, COLS) for part in (gate_weight.T, up_weight.T, down_weight)], axis=1
    )
    dma = pltpu.SemaphoreType.DMA
    vmem = pltpu.VMEM
    hbm = pl.BlockSpec(memory_space=pl.ANY)
    tangent, curvature = pl.pallas_call(
        kernel,
        out_shape=(
            jax.ShapeDtypeStruct((2, BLOCK, COLS), BF16),
            jax.ShapeDtypeStruct((2, BLOCK), F32),
        ),
        in_specs=[pl.BlockSpec(memory_space=pltpu.SMEM), hbm, hbm, hbm],
        out_specs=(pl.BlockSpec(memory_space=pltpu.VMEM), pl.BlockSpec(memory_space=pltpu.VMEM)),
        scratch_shapes=[
            vmem((2, 4, 4, 2, 16, D), BF16),
            vmem((4, 4, 3 * UNITS, COLS), BF16),
            vmem((6, UNITS, D), BF16),
            vmem((9, 4 * BLOCK, UNITS), F32),
            vmem((3, 4 * BLOCK, UNITS), BF16),
            vmem((4, 2, 4 * BLOCK, COLS), BF16),
            vmem((4, 2, 4 * BLOCK, COLS), BF16),
            vmem((4, 2, 4 * BLOCK, COLS), BF16),
            vmem((2, 2, 2, 4 * BLOCK, COLS), BF16),
            vmem((7, BLOCK, COLS), BF16),
            vmem((2, 4, 4 * BLOCK, COLS), BF16),
            vmem((2, 4, 4 * BLOCK, COLS), BF16),
            vmem((2, 4, 4 * BLOCK, COLS), BF16),
            vmem((2, 2, 4, 4, 64, COLS), BF16),
            vmem((3, BLOCK, COLS), BF16),
            vmem((3, 8, 4 * BLOCK), F32),
            vmem((8, 4 * BLOCK), F32),
            vmem((3, 8, 4 * BLOCK), F32),
            vmem((7, 8, BLOCK), F32),
            dma((3,)),
            dma((2, 3)), dma((2, 3)),
            dma((2, 4, 3)), dma((2, 4, 3)),
            dma((2, 3)), dma((2, 3)),
            dma((3, 4)), dma((3, 4)),
            dma((3,)), dma((3,)),
            dma((2, 4)), dma((2, 4)),
            dma((2, 2, 2)), dma((2, 2, 2)),
            dma((7,)), dma((7,)),
            dma((2, 2, 4)), dma((2, 2, 4)),
            dma((3,)), dma((3,)),
            dma((1,)), dma((1,)),
            dma((3,)), dma((3,)),
            dma((7,)), dma((7,)),
        ],
        name="curvature_probes",
        cost_estimate=pl.CostEstimate(flops=13 * 2 * 512 * D * UNITS, bytes_accessed=4 * 2**20, transcendentals=512 * UNITS),
        compiler_params=pltpu.CompilerParams(
            collective_id=0, has_side_effects=True, vmem_limit_bytes=60 * 2**20
        ),
    )(
        probe_seeds,
        tokens.reshape(4, 2, 16, D),
        cotangent.reshape(4, 2, 16, D),
        weights,
    )
    return tangent, curvature


def solution(mesh):
    return jax.shard_map(
        on_device,
        mesh=mesh,
        in_specs=(
            P("dp", None),
            P("dp", None),
            P("dp", ("tensor", "probe")),
            P("dp", ("tensor", "probe")),
            P(("tensor", "probe"), "dp"),
            P(),
        ),
        out_specs=(P(None, "dp", ("tensor", "probe")), P(None, "dp")),
        check_vma=False,
    )
```

time: 183 us -> 138 us (0.75)
  Pallas kernels: 175 us -> 129 us
    pallas_call x1, Pallas kernels: 175 us -> 129 us  [on_device(): pl.pallas_call(kernel, out_shape=(jax.ShapeDtypeStruct((2, BLOCK, COLS),...]
where the time goes in v2:
time: 138 us; the launch traced here: 136 us
  Pallas kernels  129 us (93%)
  local copies, waits for them, and re-layouts  5.23 us (4%)
    pallas_call x1, Pallas kernels, on_device(): pl.pallas_call(kernel, out_shape=(jax.ShapeDtypeStruct((2, BLOCK, COLS),...  129 us

profile of v2, /device:TPU:8, one launch (start us, length us, event | category | flops | bytes accessed | tf_op | source)
XLA Modules:
  0.0 136.2 jit_solution(11577544401230983450)
XLA Ops:
  0.6 0.0 copy-start
  0.6 1.3 copy.8
  1.9 1.2 copy.9
  3.1 0.0 copy-done
  3.2 1.2 pad_maximum_fusion.wa
  4.3 129.2 %curvature_probes.1 = (bf16[2,128,256]{2,1,0:T(8,128)(2,1)}, f32[2,128]{1,0:T(2,128)}) custom-call(s32[2]{0:T(128)} %seeds.1, bf16[4,2,16,4096]{3,2,1,0:T(8,128)(2,1)} %bitcast.12, bf16[4,2,16,4096]{3,2,1,0:T(8,128)(2,1)} %bitcast.13, bf16[4,672,256]{2,1,0:T(8,128)(2,1)} %pad_maximum_fusion.wa), custom_call_target="tpu_custom_call" | custom-call | flops 12213813248 | bytes 4194304 | tf_op jit(solution)/shard_map/curvature_probes/pallas_call | solution.py:496
  133.5 1.6 %copy.12 = bf16[2,128,256]{2,1,0:T(8,128)(2,1)} copy(bf16[2,128,256]{2,1,0:T(8,128)(2,1)} %get-tuple-element.4) | data formatting | bytes 262144
  135.1 1.2 copy.13
Async XLA Ops:
  0.6 2.5 %copy-start = (bf16[896,256]{1,0:T(8,128)(2,1)S(1)}, bf16[896,256]{1,0:T(8,128)(2,1)}, u32[]{:S(2)}) copy-start(bf16[896,256]{1,0:T(8,128)(2,1)} %param.10) | copy-start | bytes 1376260

commit v3 on v2

v3 whole, which is shorter than its diff:
```python
import functools

import jax
import jax.numpy as jnp
import numpy as np
from jax import lax
from jax.experimental import pallas as pl
from jax.experimental.pallas import tpu as pltpu
from jax.sharding import PartitionSpec as P

D = 4096
FF = 14336
UNITS = 224
COLS = 256
BLOCK = 128
MESH = pl.DeviceIdType.MESH
NT = (((1,), (1,)), ((), ()))
BF16, F32, I32 = jnp.bfloat16, jnp.float32, jnp.int32
IN_FACTOR = float(D**-0.5)
OUT_FACTOR = float(FF**-0.5)
OUT_FACTOR_LOW = float(np.asarray(FF**-0.5, np.float32).astype(jnp.bfloat16))
PARTS = ((0, 2 * UNITS), (2 * UNITS, UNITS))


def wrap(value):
    return np.int32((int(value) + 2**31) % 2**32 - 2**31)


STEP = -1640531535


def kernel(
    seeds, tok, cot, gate, up, down, out, curv,
    wide, wa, tc, w, dirs, acc, hid, cs0, cr0, s0, xr0, zr0, cs1, cr1, s1, zr1, xr1, cv, cvc, cvx, cvz,
    loc_sem, a2a_s, a2a_r, ag_s, ag_r, tz_s, tz_r, tx_s, tx_r, tcc_s, tcc_r,
    c_s, c_r, x0_s, x0_r, z_s, z_r, x1_s, x1_r, vc_s, vc_r, vx_s, vx_r, vz_s, vz_r,
):
    dp, tensor, core = lax.axis_index("dp"), lax.axis_index("tensor"), lax.axis_index("probe")
    zh, y = dp // 4, dp % 4
    zl, x = tensor // 4, tensor % 4

    def dev_z(step):
        z = (zh * 2 + zl + step) % 8
        return ((z // 2) * 4 + y, (z % 2) * 4 + x, core)

    def dev_y(step):
        return (zh * 4 + (y + step) % 4, tensor, core)

    def dev_x(step):
        return (dp, zl * 4 + (x + step) % 4, core)

    dev_c = (dp, tensor, 1 - core)

    def remote(src, dst, send, recv, device):
        return pltpu.make_async_remote_copy(
            src_ref=src, dst_ref=dst, send_sem=send, recv_sem=recv,
            device_id=device, device_id_type=MESH,
        )

    barrier = pltpu.get_barrier_semaphore()
    peers = [dev_z(d) for d in range(1, 8)] + [dev_x(d) for d in range(1, 4)] + [dev_y(1), dev_y(3), dev_c]
    for peer in peers:
        pl.semaphore_signal(barrier, inc=1, device_id=peer, device_id_type=MESH)
    local = [
        pltpu.make_async_copy(tok, tc.at[0, zh], loc_sem.at[0]),
        pltpu.make_async_copy(cot, tc.at[1, zh], loc_sem.at[1]),
        pltpu.make_async_copy(down, wa.at[:, pl.ds(2 * UNITS, UNITS)], loc_sem.at[2]),
        pltpu.make_async_copy(gate, wide.at[0], loc_sem.at[3]),
        pltpu.make_async_copy(up, wide.at[1], loc_sem.at[4]),
    ]
    for k in (3, 4, 2, 0, 1):
        local[k].start()
    for k in range(2):
        local[3 + k].wait()
        wa[:, pl.ds(k * UNITS, UNITS), :] = wide[k].T.reshape(4, UNITS, COLS)
    local[2].wait()
    w[y, zh] = wa[zh]
    pl.semaphore_wait(barrier, len(peers))

    started = []

    def go(copy):
        copy.start()
        started.append(copy)

    def w_at(part, yy, j):
        lo, n = PARTS[part]
        return w.at[yy % 4, (zh + j) % 4, pl.ds(lo, n)]

    def ag_send(part, j):
        lo, n = PARTS[part]
        src = wa.at[zh, pl.ds(lo, n)] if j == 0 else w_at(part, y, j)
        go(remote(src, w_at(part, y, j), ag_s.at[part, j, 0], ag_r.at[part, j, 0], dev_y(1)))
        go(remote(src, w_at(part, y, j), ag_s.at[part, j, 1], ag_r.at[part, j, 1], dev_y(3)))

    def ag_wait(part, j, side, source):
        ref = w_at(part, source, j)
        remote(ref, ref, ag_s.at[part, j, side], ag_r.at[part, j, side], dev_y(1)).wait_recv()

    def ag_relay(part, j):
        side, source, onward = (0, y + 3, 1) if j % 2 == 0 else (1, y + 1, 3)
        ag_wait(part, j, side, source)
        ref = w_at(part, source, j)
        go(remote(ref, ref, ag_s.at[part, j, 2], ag_r.at[part, j, 2], dev_y(onward)))

    def ag_finish(part, j):
        side, source = (1, y + 1) if j % 2 == 0 else (0, y + 3)
        ag_wait(part, j, side, source)
        ag_wait(part, j, 2, y + 2)

    def a2a_send(part, d):
        lo, n = PARTS[part]
        target = (zh + d) % 4
        go(remote(wa.at[target, pl.ds(lo, n)], w_at(part, y, 0), a2a_s.at[part, d - 1], a2a_r.at[part, 3 - d], dev_z(2 * d)))

    def a2a_wait(part, j):
        ref = w_at(part, y, j)
        remote(ref, ref, a2a_s.at[part, j - 1], a2a_r.at[part, j - 1], dev_z(2)).wait_recv()

    HALF = (pl.ds(0, D // 2), pl.ds(D // 2, D // 2))

    def tz(up, k, block, own=False):
        side, m = 0 if up else 1, k % 2
        dst = tc.at[m, block % 4, x, core]
        src = (tok, cot)[m].at[x, core] if own else dst
        if k > 1:
            dst = dst.at[:, HALF[side]]
            src = dst
        return remote(src, dst, tz_s.at[side, k], tz_r.at[side, k], dev_z(1 if up else 7))

    def tz_block(up, k):
        return zh + 2 if k > 1 else zh + 3 if up else zh + 1

    def tz_wait(up, k):
        tz(up, k, tz_block(up, k)).wait_recv()

    def tz_open(k):
        for up in (True, False):

            @pl.when(zl == (1 if up else 0))
            def _():
                tz(up, k, zh, own=True).start()

    def tz_pass(k):
        for up in (True, False):

            @pl.when(zl == (0 if up else 1))
            def _():
                tz_wait(up, k)
                tz(up, k, tz_block(up, k)).start()

    def tz_half(m):
        for up in (True, False):

            @pl.when(zl == (1 if up else 0))
            def _():
                tz_wait(up, m)
                tz(up, m + 2, tz_block(up, m)).start()

    def tz_rest(k):
        for up in (True, False):

            @pl.when(zl == (1 if up else 0))
            def _():
                tz_wait(up, k)

    def tx(j, m, side, source=0):
        ref = tc.at[m, (zh + j) % 4, (x + source) % 4, core]
        return remote(ref, ref, tx_s.at[j - 1, m, side], tx_r.at[j - 1, m, side], dev_x(1 if side == 0 else 3))

    def tx_onward(j, m, side, source):
        ref = tc.at[m, (zh + j) % 4, (x + source) % 4, core, :, HALF[side]]
        return remote(ref, ref, tx_s.at[j - 1, m, 2 + side], tx_r.at[j - 1, m, 2 + side], dev_x(1 if side == 0 else 3))

    def tx_send(m, *js):
        for j in js:
            go(tx(j, m, 0))
            go(tx(j, m, 1))

    def tx_relay(m, *js):
        for j in js:
            for side, source in ((0, 3), (1, 1)):
                tx(j, m, side, source).wait_recv()
                go(tx_onward(j, m, side, source))

    def tok_share(m, *js):
        for j in js:
            for side in range(2):
                tx_onward(j, m, side, 2).wait_recv()
            ref = tc.at[m, (zh + j) % 4, :, core]
            go(remote(ref, ref, tcc_s.at[m, j - 1], tcc_r.at[m, j - 1], dev_c))

    def tok_finish(m):
        for j in (1, 3, 2):
            ref = tc.at[m, (zh + j) % 4, :, 1 - core]
            remote(ref, ref, tcc_s.at[m, j - 1], tcc_r.at[m, j - 1], dev_c).wait_recv()
        local[m].wait()

    first_unit = (tensor * 2 + core) * (4 * UNITS) + zh * UNITS

    def make_signs_of(m, lo, hi):
        unit_mul, feature_mul = (wrap(STEP), wrap(STEP * FF)) if m < 2 else (wrap(STEP * D), wrap(STEP))
        base = (
            lax.broadcasted_iota(I32, (16, D), 0) * unit_mul + lax.broadcasted_iota(I32, (16, D), 1) * feature_mul
        )

        def body(i, _):
            start = (first_unit + i * 16) * unit_mul + np.int32(40503 * (m + 1))
            for p in range(2):
                u = base + (start + seeds[p])
                u = u ^ lax.shift_right_logical(u, np.int32(16))
                u = u * np.int32(739982445)
                u = u ^ lax.shift_right_logical(u, np.int32(13))
                u = u * np.int32(695872825)
                dirs[2 * m + p, pl.ds(pl.multiple_of(i * 16, 16), 16), :] = jnp.where(u < 0, -1.0, 1.0).astype(BF16)
            return 0

        lax.fori_loop(lo, hi, body, 0)

    made = [0]

    def make_signs(n):
        while n:
            m, lo = divmod(made[0], 14)
            take = min(n, 14 - lo)
            make_signs_of(m, lo, lo + take)
            made[0] += take
            n -= take

    def rows_of(m, lo, n):
        return tc[m, pl.ds(lo, n)].reshape(n * BLOCK, D)

    def dir_body(i, _):
        acc[i] = lax.dot_general(rows_of(i // 4, 0, 4), dirs[i], NT, preferred_element_type=F32)
        return 0

    ag_send(0, 0)
    a2a_send(0, 1)
    a2a_send(0, 3)
    tz_open(0)
    tz_open(1)
    ag_send(1, 0)
    make_signs(15)
    ag_relay(0, 0)
    make_signs(14)
    ag_relay(1, 0)
    for j in (1, 3):
        a2a_wait(0, j)
        ag_send(0, j)
    make_signs(3)
    tz_pass(0)
    make_signs(4)
    tz_half(0)
    tx_send(0, 1, 3)
    tz_pass(1)
    make_signs(3)
    tz_pass(2)
    tz_half(1)
    make_signs(3)
    tz_rest(2)
    tx_send(0, 2)
    tz_pass(3)
    a2a_send(0, 2)
    a2a_send(1, 1)
    a2a_send(1, 3)
    a2a_send(1, 2)
    tx_relay(0, 1, 3)
    tx_relay(0, 2)
    tx_send(1, 1, 3)
    tz_rest(3)
    tx_send(1, 2)
    for j in (1, 3):
        ag_relay(0, j)
    tok_share(0, 1, 3, 2)
    tok_finish(0)
    lax.fori_loop(0, 2, dir_body, 0)
    tx_relay(1, 1, 3)
    for j in (2,):
        a2a_wait(0, j)
        ag_send(0, j)
    lax.fori_loop(2, 4, dir_body, 0)
    tx_relay(1, 2)
    ag_relay(0, 2)
    for j in (1, 3, 2):
        a2a_wait(1, j)
        ag_send(1, j)
    tok_share(1, 1, 3, 2)
    tok_finish(1)
    lax.fori_loop(4, 6, dir_body, 0)
    for j in (1, 3):
        ag_relay(1, j)
    for j in (0, 1, 3, 2):
        ag_finish(0, j)

    def plain(i, _):
        rhs = jnp.concatenate([w[b % 4, b // 4, pl.ds(i * UNITS, UNITS), :] for b in range(16)], axis=1)
        acc[6 + i] = lax.dot_general(rows_of(i // 2, 0, 4), rhs, NT, preferred_element_type=F32)
        return 0

    lax.fori_loop(0, 2, plain, 0)
    ag_relay(1, 2)

    def point(i, _):
        r = pl.ds(pl.multiple_of(i * 32, 32), 32)
        gate, up = acc[6, r, :], acc[7, r, :]
        s = jax.nn.sigmoid(gate)
        silu = gate * s
        slope = s * (1.0 + gate * (1.0 - s))
        bend = s * (1.0 - s) * (2.0 + gate * (1.0 - 2.0 * s))
        hid[2, r, :] = (silu * up).astype(BF16)
        for p in range(2):
            gd, ud = acc[p, r, :] * IN_FACTOR, acc[2 + p, r, :] * IN_FACTOR
            hd = slope * gd * up + silu * ud
            hid[p, r, :] = hd.astype(BF16)
            acc[2 + p, r, :] = hd
            acc[p, r, :] = bend * gd * gd * up + 2.0 * slope * gd * ud
        return 0

    lax.fori_loop(0, 16, point, 0)
    for j in (0, 1, 3, 2):
        ag_finish(1, j)

    def curvature_terms():
        cv[0] = jnp.zeros((8, 4 * BLOCK), F32)
        for p in range(2):
            terms = acc[8] * acc[p] + (2.0 * OUT_FACTOR_LOW) * acc[4 + p] * acc[2 + p]
            cv[0, pl.ds(p, 1), :] = jnp.sum(terms.T, axis=0, keepdims=True) * OUT_FACTOR
        go(remote(cv.at[0], cvc, vc_s.at[0], vc_r.at[0], dev_c))

    def columns(e, lr, other):
        return (((zl + lr) % 2) * 4 + (x + e) % 4) * 2 + other

    def tangent(p, b):
        col = pl.ds(pl.multiple_of(b * COLS, COLS), COLS)
        one = jnp.dot(hid[p], w[b % 4, b // 4, pl.ds(2 * UNITS, UNITS), :], preferred_element_type=F32)
        two = jnp.dot(hid[2], dirs[4 + p, :, col], preferred_element_type=F32)
        return one + two * OUT_FACTOR_LOW

    def column(p, g, i, side):
        return columns((i - x) % 4, g, side) if p else columns(g, i, side)

    def give(p, g):
        out_ref, in_ref = (cs1, cr1) if p else (cs0, cr0)
        return remote(out_ref.at[g], in_ref.at[g], c_s.at[p, g], c_r.at[p, g], dev_c)

    def theirs(p, g):
        n, out_ref = (4, cs1) if p else (2, cs0)

        def body(i, _):
            out_ref[g, pl.ds(i, 1)] = tangent(p, column(p, g, i, 1 - core)).astype(BF16)[None]
            return 0

        lax.fori_loop(0, n, body, 0)
        go(give(p, g))

    def ours(p, g):
        n, mine, in_ref = (4, s1, cr1) if p else (2, s0, cr0)
        give(p, g).wait_recv()

        def body(i, _):
            total = tangent(p, column(p, g, i, core)) + in_ref[g, i].astype(F32)
            mine[g, pl.ds(i, 1)] = total.astype(BF16)[None]
            return 0

        lax.fori_loop(0, n, body, 0)

    def z_rows(d, u):
        return pl.ds(pl.multiple_of((((zh * 2 + zl + d) % 8) // 2) * BLOCK + u * 64, 64), 64)

    def z_part(p, up, u, d):
        far = d if up else 8 - d
        rows = z_rows(far, u)
        return s1.at[far % 2, :, rows] if p else s0.at[0, pl.ds(far % 2, 1), rows]

    def z_hop(p, up, u, d):
        side = 0 if up else 1
        land = (zr1 if p else zr0).at[side, u, d - 1]
        return remote(
            z_part(p, up, u, d), land, z_s.at[p, side, u, d - 1], z_r.at[p, side, u, d - 1], dev_z(1 if up else 7)
        )

    def z_add(p, up, u, d):
        z_hop(p, up, u, d).wait_recv()
        far = (d - 1 if up else 9 - d) % 8
        side, r = 0 if up else 1, z_rows(far, u)
        if p:

            def body(i, _):
                s1[far % 2, i, r, :] = (s1[far % 2, i, r, :].astype(F32) + zr1[side, u, d - 1, i].astype(F32)).astype(BF16)
                return 0

            lax.fori_loop(0, 4, body, 0)
        else:
            s0[0, far % 2, r, :] = (s0[0, far % 2, r, :].astype(F32) + zr0[side, u, d - 1, 0].astype(F32)).astype(BF16)

    def z_open(p, d):
        go(z_hop(p, True, 4 - d, d))
        go(z_hop(p, False, d - 3, d))

    def z_lead(p, d):
        for up in (True, False):
            lane = 0 if up else 1
            z_add(p, up, lane, d + 1)
            go(z_hop(p, up, lane, d))

    def z_lag(p, d):
        for up in (True, False):
            lane = 1 if up else 0
            z_add(p, up, lane, d + 1)
            go(z_hop(p, up, lane, d))

    def z_end(p):
        for up in (True, False):
            for u in range(2):
                z_add(p, up, u, 1)

    def x_hop(up, u, d):
        side = 0 if up else 1
        e = d if up else 4 - d
        return remote(s0.at[e, u], xr0.at[side, u, d - 1], x0_s.at[side, u, d - 1], x0_r.at[side, u, d - 1], dev_x(1 if up else 3))

    def x_add(up, u, d):
        x_hop(up, u, d).wait_recv()
        e = (d - 1 if up else 5 - d) % 4

        def body(i, _):
            r = pl.ds(pl.multiple_of(i * 64, 64), 64)
            s0[e, u, r, :] = (s0[e, u, r, :].astype(F32) + xr0[0 if up else 1, u, d - 1, r, :].astype(F32)).astype(BF16)
            return 0

        lax.fori_loop(0, 8, body, 0)

    theirs(0, 2)
    theirs(1, 0)
    ours(0, 2)
    go(x_hop(True, 0, 2))
    go(x_hop(False, 1, 2))
    theirs(1, 1)
    ours(1, 0)
    z_open(1, 4)
    theirs(0, 1)
    ours(1, 1)
    z_open(1, 3)
    theirs(0, 3)
    ours(0, 1)
    go(x_hop(True, 1, 1))
    ours(0, 3)
    go(x_hop(False, 0, 1))
    x_add(True, 0, 2)
    go(x_hop(True, 0, 1))
    x_add(False, 1, 2)
    go(x_hop(False, 1, 1))
    theirs(0, 0)
    z_lead(1, 3)
    ours(0, 0)
    z_lag(1, 2)
    lax.fori_loop(2, 3, plain, 0)
    z_lead(1, 2)
    z_lag(1, 1)
    curvature_terms()
    z_lead(1, 1)
    for lr in range(2):
        x_add(True, lr, 1)
        x_add(False, lr, 1)
    z_open(0, 4)
    z_open(0, 3)
    remote(cvc, cvc, vc_s.at[0], vc_r.at[0], dev_c).wait_recv()
    cv[1] = cv[0] + cvc[...]
    for d in range(1, 4):
        go(remote(cv.at[1], cvx.at[d - 1], vx_s.at[d - 1], vx_r.at[d - 1], dev_x(d)))
    z_end(1)
    z_lead(0, 3)

    def x_copy(e):
        return remote(
            s1.at[0, (x + e) % 4, pl.ds(pl.multiple_of(zh * BLOCK, BLOCK), BLOCK)], xr1.at[e - 1], x1_s.at[e - 1], x1_r.at[e - 1], dev_x(e)
        )

    for e in range(1, 4):
        go(x_copy(e))
    z_lag(0, 2)
    z_lead(0, 2)
    for d in range(1, 4):
        remote(cv.at[1], cvx.at[d - 1], vx_s.at[d - 1], vx_r.at[d - 1], dev_x(d)).wait_recv()
    cv[2] = (cv[1] + cvx[0]) + (cvx[1] + cvx[2])
    for d in range(1, 8):
        zz = ((zh * 2 + zl + d) % 8) // 2
        src = cv.at[2, :, pl.ds(pl.multiple_of(zz * BLOCK, BLOCK), BLOCK)]
        go(remote(src, cvz.at[d - 1], vz_s.at[d - 1], vz_r.at[d - 1], dev_z(d)))
    z_lag(0, 1)
    z_lead(0, 1)

    for d in range(1, 8):
        remote(cvz.at[d - 1], cvz.at[d - 1], vz_s.at[d - 1], vz_r.at[d - 1], dev_z(d)).wait_recv()
    total = cv[2, :, pl.ds(pl.multiple_of(zh * BLOCK, BLOCK), BLOCK)]
    for d in range(7):
        total = total + cvz[d]
    curv[...] = total[:2]

    z_end(0)
    for e in range(1, 4):
        x_copy(e).wait_recv()

    def last(i, _):
        r = pl.ds(pl.multiple_of(i * 32, 32), 32)
        own = pl.ds(pl.multiple_of(zh * BLOCK + i * 32, 32), 32)
        out[0, r, :] = s0[0, 0, own, :]
        total = s1[0, x, own, :].astype(F32)
        for e in range(3):
            total = total + xr1[e, r, :].astype(F32)
        out[1, r, :] = total.astype(BF16)
        return 0

    lax.fori_loop(0, 4, last, 0)
    for up in (True, False):
        for k in range(4):
            tz(up, k, tz_block(up, k)).wait_send()
    for copy in started:
        copy.wait_send()


def on_device(tokens, cotangent, gate_weight, up_weight, down_weight, probe_seeds):
    dma = pltpu.SemaphoreType.DMA
    vmem = pltpu.VMEM
    hbm = pl.BlockSpec(memory_space=pl.ANY)
    tangent, curvature = pl.pallas_call(
        kernel,
        out_shape=(
            jax.ShapeDtypeStruct((2, BLOCK, COLS), BF16),
            jax.ShapeDtypeStruct((2, BLOCK), F32),
        ),
        in_specs=[pl.BlockSpec(memory_space=pltpu.SMEM), hbm, hbm, hbm, hbm, hbm],
        out_specs=(pl.BlockSpec(memory_space=pltpu.VMEM), pl.BlockSpec(memory_space=pltpu.VMEM)),
        scratch_shapes=[
            vmem((2, COLS, 4 * UNITS), BF16),
            vmem((4, 3 * UNITS, COLS), BF16),
            vmem((2, 4, 4, 2, 16, D), BF16),
            vmem((4, 4, 3 * UNITS, COLS), BF16),
            vmem((6, UNITS, D), BF16),
            vmem((9, 4 * BLOCK, UNITS), F32),
            vmem((3, 4 * BLOCK, UNITS), BF16),
            vmem((4, 2, 4 * BLOCK, COLS), BF16),
            vmem((4, 2, 4 * BLOCK, COLS), BF16),
            vmem((4, 2, 4 * BLOCK, COLS), BF16),
            vmem((2, 2, 2, 4 * BLOCK, COLS), BF16),
            vmem((2, 2, 4, 1, 64, COLS), BF16),
            vmem((2, 4, 4 * BLOCK, COLS), BF16),
            vmem((2, 4, 4 * BLOCK, COLS), BF16),
            vmem((2, 4, 4 * BLOCK, COLS), BF16),
            vmem((2, 2, 4, 4, 64, COLS), BF16),
            vmem((3, BLOCK, COLS), BF16),
            vmem((3, 8, 4 * BLOCK), F32),
            vmem((8, 4 * BLOCK), F32),
            vmem((3, 8, 4 * BLOCK), F32),
            vmem((7, 8, BLOCK), F32),
            dma((5,)),
            dma((2, 3)), dma((2, 3)),
            dma((2, 4, 3)), dma((2, 4, 3)),
            dma((2, 4)), dma((2, 4)),
            dma((3, 2, 4)), dma((3, 2, 4)),
            dma((2, 3)), dma((2, 3)),
            dma((2, 4)), dma((2, 4)),
            dma((2, 2, 2)), dma((2, 2, 2)),
            dma((2, 2, 2, 4)), dma((2, 2, 2, 4)),
            dma((3,)), dma((3,)),
            dma((1,)), dma((1,)),
            dma((3,)), dma((3,)),
            dma((7,)), dma((7,)),
        ],
        name="curvature_probes",
        cost_estimate=pl.CostEstimate(flops=13 * 2 * 512 * D * UNITS, bytes_accessed=4 * 2**20, transcendentals=512 * UNITS),
        compiler_params=pltpu.CompilerParams(
            collective_id=0, has_side_effects=True, vmem_limit_bytes=60 * 2**20
        ),
    )(
        probe_seeds,
        tokens.reshape(4, 2, 16, D),
        cotangent.reshape(4, 2, 16, D),
        gate_weight,
        up_weight,
        down_weight.reshape(4, UNITS, COLS),
    )
    return tangent, curvature


def solution(mesh):
    return jax.shard_map(
        on_device,
        mesh=mesh,
        in_specs=(
            P("dp", None),
            P("dp", None),
            P("dp", ("tensor", "probe")),
            P("dp", ("tensor", "probe")),
            P(("tensor", "probe"), "dp"),
            P(),
        ),
        out_specs=(P(None, "dp", ("tensor", "probe")), P(None, "dp")),
        check_vma=False,
    )
```

time: 138 us -> 123 us (0.89); the launches traced: 136 us -> 123 us
  Pallas kernels: 129 us -> 120 us
  local copies, waits for them, and re-layouts: 5.23 us -> 2.13 us
    pallas_call x1, Pallas kernels: 129 us -> 120 us  [on_device(): pl.pallas_call(kernel, out_shape=(jax.ShapeDtypeStruct((2, BLOCK, COLS),...]
    transpose x2 -> x0, local copies, waits for them, and re-layouts: 2.5 us -> none  [on_device(): weights = jnp.concatenate([part.reshape(4, UNITS, COLS) for part in (gate...]
where the time goes in v3:
time: 123 us
  Pallas kernels  120 us (98%)
  local copies, waits for them, and re-layouts  2.13 us (2%)
    pallas_call x1, Pallas kernels, on_device(): pl.pallas_call(kernel, out_shape=(jax.ShapeDtypeStruct((2, BLOCK, COLS),...  120 us

profile of v3, /device:TPU:8, one launch (start us, length us, event | category | flops | bytes accessed | tf_op | source)
XLA Modules:
  0.0 123.3 jit_solution(8274131175008581218)
XLA Ops:
  0.6 120.5 %curvature_probes.1 = (bf16[2,128,256]{2,1,0:T(8,128)(2,1)}, f32[2,128]{1,0:T(2,128)}) custom-call(s32[2]{0:T(128)} %seeds.1, bf16[4,2,16,4096]{3,2,1,0:T(8,128)(2,1)} %bitcast.3, bf16[4,2,16,4096]{3,2,1,0:T(8,128)(2,1)} %bitcast.4, bf16[256,896]{1,0:T(8,128)(2,1)} %gate.1, bf16[256,896]{1,0:T(8,128)(2,1)} %up.1, bf16[4,224,256]{2,1,0:T(8,128)(2,1)} %bitcast.5), custom_call_target="tpu_custom_call" | custom-call | flops 12213813248 | bytes 4194304 | tf_op jit(solution)/shard_map/curvature_probes/pallas_call | solution.py:526
  121.1 0.0 copy-start
  121.1 1.6 %copy.10 = bf16[2,128,256]{2,1,0:T(8,128)(2,1)} copy(bf16[2,128,256]{2,1,0:T(8,128)(2,1)} %get-tuple-element.4) | data formatting | bytes 262144
  122.7 0.0 copy-done
  122.7 0.6 copy.11
Async XLA Ops:
  121.1 1.6 %copy-start = (f32[2,128]{1,0:T(2,128)S(1)}, f32[2,128]{1,0:T(2,128)}, u32[]{:S(2)}) copy-start(f32[2,128]{1,0:T(2,128)} %get-tuple-element.5) | copy-start | bytes 3076

commit v4 on v3

--- a/solution.py
+++ b/solution.py
@@ -237,58 +237,53 @@
     ag_send(0, 0)
     a2a_send(0, 1)
     a2a_send(0, 3)
+    a2a_send(0, 2)
     tz_open(0)
     tz_open(1)
     ag_send(1, 0)
     make_signs(15)
     ag_relay(0, 0)
-    make_signs(14)
-    ag_relay(1, 0)
+    make_signs(6)
     for j in (1, 3):
         a2a_wait(0, j)
         ag_send(0, j)
-    make_signs(3)
     tz_pass(0)
-    make_signs(4)
+    tz_pass(1)
+    ag_relay(1, 0)
+    make_signs(9)
     tz_half(0)
     tx_send(0, 1, 3)
-    tz_pass(1)
-    make_signs(3)
+    tz_half(1)
+    a2a_wait(0, 2)
+    ag_send(0, 2)
+    make_signs(6)
+    for j in (1, 3):
+        ag_relay(0, j)
     tz_pass(2)
-    tz_half(1)
-    make_signs(3)
+    tz_pass(3)
+    for d in (1, 3, 2):
+        a2a_send(1, d)
+    make_signs(6)
     tz_rest(2)
     tx_send(0, 2)
-    tz_pass(3)
-    a2a_send(0, 2)
-    a2a_send(1, 1)
-    a2a_send(1, 3)
-    a2a_send(1, 2)
     tx_relay(0, 1, 3)
     tx_relay(0, 2)
     tx_send(1, 1, 3)
+    ag_relay(0, 2)
+    tok_share(0, 1, 3, 2)
     tz_rest(3)
     tx_send(1, 2)
+    tok_finish(0)
+    lax.fori_loop(0, 1, dir_body, 0)
     for j in (1, 3):
-        ag_relay(0, j)
-    tok_share(0, 1, 3, 2)
-    tok_finish(0)
-    lax.fori_loop(0, 2, dir_body, 0)
-    tx_relay(1, 1, 3)
-    for j in (2,):
-        a2a_wait(0, j)
-        ag_send(0, j)
-    lax.fori_loop(2, 4, dir_body, 0)
-    tx_relay(1, 2)
-    ag_relay(0, 2)
-    for j in (1, 3, 2):
         a2a_wait(1, j)
         ag_send(1, j)
-    tok_share(1, 1, 3, 2)
-    tok_finish(1)
-    lax.fori_loop(4, 6, dir_body, 0)
-    for j in (1, 3):
-        ag_relay(1, j)
+    tx_relay(1, 1, 3)
+    lax.fori_loop(1, 3, dir_body, 0)
+    a2a_wait(1, 2)
+    ag_send(1, 2)
+    tx_relay(1, 2)
+    lax.fori_loop(3, 4, dir_body, 0)
     for j in (0, 1, 3, 2):
         ag_finish(0, j)
 
@@ -298,7 +293,9 @@
         return 0
 
     lax.fori_loop(0, 2, plain, 0)
-    ag_relay(1, 2)
+    for j in (1, 3):
+        ag_relay(1, j)
+    tok_share(1, 1, 3, 2)
 
     def point(i, _):
         r = pl.ds(pl.multiple_of(i * 32, 32), 32)
@@ -317,6 +314,9 @@
         return 0
 
     lax.fori_loop(0, 16, point, 0)
+    ag_relay(1, 2)
+    tok_finish(1)
+    lax.fori_loop(4, 6, dir_body, 0)
     for j in (0, 1, 3, 2):
         ag_finish(1, j)
 

time: 123 us -> 121 us (0.984)
  Pallas kernels: 120 us -> 118 us
    pallas_call x1, Pallas kernels: 120 us -> 118 us  [on_device(): pl.pallas_call(kernel, out_shape=(jax.ShapeDtypeStruct((2, BLOCK, COLS),...]
where the time goes in v4:
time: 121 us
  Pallas kernels  118 us (98%)
  local copies, waits for them, and re-layouts  2.13 us (2%)
    pallas_call x1, Pallas kernels, on_device(): pl.pallas_call(kernel, out_shape=(jax.ShapeDtypeStruct((2, BLOCK, COLS),...  118 us

profile of v4, /device:TPU:8, one launch (start us, length us, event | category | flops | bytes accessed | tf_op | source)
XLA Modules:
  0.0 120.7 jit_solution(6391124139889684215)
XLA Ops:
  0.6 118.0 %curvature_probes.1 = (bf16[2,128,256]{2,1,0:T(8,128)(2,1)}, f32[2,128]{1,0:T(2,128)}) custom-call(s32[2]{0:T(128)} %seeds.1, bf16[4,2,16,4096]{3,2,1,0:T(8,128)(2,1)} %bitcast.3, bf16[4,2,16,4096]{3,2,1,0:T(8,128)(2,1)} %bitcast.4, bf16[256,896]{1,0:T(8,128)(2,1)} %gate.1, bf16[256,896]{1,0:T(8,128)(2,1)} %up.1, bf16[4,224,256]{2,1,0:T(8,128)(2,1)} %bitcast.5), custom_call_target="tpu_custom_call" | custom-call | flops 12213813248 | bytes 4194304 | tf_op jit(solution)/shard_map/curvature_probes/pallas_call | solution.py:526
  118.6 0.0 copy-start
  118.6 1.6 %copy.10 = bf16[2,128,256]{2,1,0:T(8,128)(2,1)} copy(bf16[2,128,256]{2,1,0:T(8,128)(2,1)} %get-tuple-element.4) | data formatting | bytes 262144
  120.2 0.0 copy-done
  120.2 0.6 copy.11
Async XLA Ops:
  118.6 1.6 %copy-start = (f32[2,128]{1,0:T(2,128)S(1)}, f32[2,128]{1,0:T(2,128)}, u32[]{:S(2)}) copy-start(f32[2,128]{1,0:T(2,128)} %get-tuple-element.5) | copy-start | bytes 3076

commit v5 on v4

--- a/solution.py
+++ b/solution.py
@@ -113,6 +113,16 @@
         target = (zh + d) % 4
         go(remote(wa.at[target, pl.ds(lo, n)], w_at(part, y, 0), a2a_s.at[part, d - 1], a2a_r.at[part, 3 - d], dev_z(2 * d)))
 
+    def a2a_far(k):
+        rows = pl.ds(k * UNITS, UNITS)
+        return remote(
+            wa.at[(zh + 2) % 4, rows], w.at[y, zh, rows], a2a_s.at[0, 1 + 2 * k], a2a_r.at[0, 1 + 2 * k], dev_z(4)
+        )
+
+    def a2a_far_wait():
+        for k in range(2):
+            a2a_far(k).wait_recv()
+
     def a2a_wait(part, j):
         ref = w_at(part, y, j)
         remote(ref, ref, a2a_s.at[part, j - 1], a2a_r.at[part, j - 1], dev_z(2)).wait_recv()
@@ -237,7 +247,7 @@
     ag_send(0, 0)
     a2a_send(0, 1)
     a2a_send(0, 3)
-    a2a_send(0, 2)
+    go(a2a_far(0))
     tz_open(0)
     tz_open(1)
     ag_send(1, 0)
@@ -254,8 +264,7 @@
     tz_half(0)
     tx_send(0, 1, 3)
     tz_half(1)
-    a2a_wait(0, 2)
-    ag_send(0, 2)
+    go(a2a_far(1))
     make_signs(6)
     for j in (1, 3):
         ag_relay(0, j)
@@ -267,6 +276,8 @@
     tz_rest(2)
     tx_send(0, 2)
     tx_relay(0, 1, 3)
+    a2a_far_wait()
+    ag_send(0, 2)
     tx_relay(0, 2)
     tx_send(1, 1, 3)
     ag_relay(0, 2)
@@ -554,7 +565,7 @@
             vmem((3, 8, 4 * BLOCK), F32),
             vmem((7, 8, BLOCK), F32),
             dma((5,)),
-            dma((2, 3)), dma((2, 3)),
+            dma((2, 4)), dma((2, 4)),
             dma((2, 4, 3)), dma((2, 4, 3)),
             dma((2, 4)), dma((2, 4)),
             dma((3, 2, 4)), dma((3, 2, 4)),

time: 121 us -> 119 us (0.983)
  Pallas kernels: 118 us -> 116 us
    pallas_call x1, Pallas kernels: 118 us -> 116 us  [on_device(): pl.pallas_call(kernel, out_shape=(jax.ShapeDtypeStruct((2, BLOCK, COLS),...]
where the time goes in v5:
time: 119 us
  Pallas kernels  116 us (97%)
  local copies, waits for them, and re-layouts  2.13 us (2%)
    pallas_call x1, Pallas kernels, on_device(): pl.pallas_call(kernel, out_shape=(jax.ShapeDtypeStruct((2, BLOCK, COLS),...  116 us

profile of v5, /device:TPU:8, one launch (start us, length us, event | category | flops | bytes accessed | tf_op | source)
XLA Modules:
  0.0 118.6 jit_solution(554691779177704712)
XLA Ops:
  0.6 115.8 %curvature_probes.1 = (bf16[2,128,256]{2,1,0:T(8,128)(2,1)}, f32[2,128]{1,0:T(2,128)}) custom-call(s32[2]{0:T(128)} %seeds.1, bf16[4,2,16,4096]{3,2,1,0:T(8,128)(2,1)} %bitcast.3, bf16[4,2,16,4096]{3,2,1,0:T(8,128)(2,1)} %bitcast.4, bf16[256,896]{1,0:T(8,128)(2,1)} %gate.1, bf16[256,896]{1,0:T(8,128)(2,1)} %up.1, bf16[4,224,256]{2,1,0:T(8,128)(2,1)} %bitcast.5), custom_call_target="tpu_custom_call" | custom-call | flops 12213813248 | bytes 4194304 | tf_op jit(solution)/shard_map/curvature_probes/pallas_call | solution.py:537
  116.4 0.0 copy-start
  116.4 1.6 %copy.10 = bf16[2,128,256]{2,1,0:T(8,128)(2,1)} copy(bf16[2,128,256]{2,1,0:T(8,128)(2,1)} %get-tuple-element.4) | data formatting | bytes 262144
  118.0 0.0 copy-done
  118.0 0.6 copy.11
Async XLA Ops:
  116.4 1.6 %copy-start = (f32[2,128]{1,0:T(2,128)S(1)}, f32[2,128]{1,0:T(2,128)}, u32[]{:S(2)}) copy-start(f32[2,128]{1,0:T(2,128)} %get-tuple-element.5) | copy-start | bytes 3076

commit v6 on v5

--- a/solution.py
+++ b/solution.py
@@ -270,7 +270,7 @@
         ag_relay(0, j)
     tz_pass(2)
     tz_pass(3)
-    for d in (1, 3, 2):
+    for d in (2, 1, 3):
         a2a_send(1, d)
     make_signs(6)
     tz_rest(2)

time: 119 us -> 120 us (level)
    pallas_call x1, Pallas kernels: 116 us -> 117 us  [on_device(): pl.pallas_call(kernel, out_shape=(jax.ShapeDtypeStruct((2, BLOCK, COLS),...]
where the time goes in v6:
time: 120 us
  Pallas kernels  117 us (98%)
  local copies, waits for them, and re-layouts  2.13 us (2%)
    pallas_call x1, Pallas kernels, on_device(): pl.pallas_call(kernel, out_shape=(jax.ShapeDtypeStruct((2, BLOCK, COLS),...  117 us

profile of v6, /device:TPU:8, one launch (start us, length us, event | category | flops | bytes accessed | tf_op | source)
XLA Modules:
  0.0 119.9 jit_solution(13008280469089634349)
XLA Ops:
  0.6 117.1 %curvature_probes.1 = (bf16[2,128,256]{2,1,0:T(8,128)(2,1)}, f32[2,128]{1,0:T(2,128)}) custom-call(s32[2]{0:T(128)} %seeds.1, bf16[4,2,16,4096]{3,2,1,0:T(8,128)(2,1)} %bitcast.3, bf16[4,2,16,4096]{3,2,1,0:T(8,128)(2,1)} %bitcast.4, bf16[256,896]{1,0:T(8,128)(2,1)} %gate.1, bf16[256,896]{1,0:T(8,128)(2,1)} %up.1, bf16[4,224,256]{2,1,0:T(8,128)(2,1)} %bitcast.5), custom_call_target="tpu_custom_call" | custom-call | flops 12213813248 | bytes 4194304 | tf_op jit(solution)/shard_map/curvature_probes/pallas_call | solution.py:537
  117.7 0.0 copy-start
  117.7 1.6 %copy.10 = bf16[2,128,256]{2,1,0:T(8,128)(2,1)} copy(bf16[2,128,256]{2,1,0:T(8,128)(2,1)} %get-tuple-element.4) | data formatting | bytes 262144
  119.3 0.0 copy-done
  119.3 0.6 copy.11
Async XLA Ops:
  117.7 1.6 %copy-start = (f32[2,128]{1,0:T(2,128)S(1)}, f32[2,128]{1,0:T(2,128)}, u32[]{:S(2)}) copy-start(f32[2,128]{1,0:T(2,128)} %get-tuple-element.5) | copy-start | bytes 3076
